TPU v7x, 512 devices: a whole 4x8x8 slice. The times are simulated.
512 devices in a mesh: blk: 128 (over x, z_hi, y, core), sub: 4 (over z_lo).
Axes of the slice: x: 4, y: 8, z: 8 (z_hi: 2, z_lo: 4; z = z_hi * 4 + z_lo), core: 2. Of those that a mesh axis runs over, the one named last changes fastest.
Arguments:
- images: bfloat16 [16384, 1152], P(('blk', 'sub')), may hold values from -0.19921875 to 0.19921875
- texts: bfloat16 [16384, 1152], P(('blk', 'sub')), may hold values from -0.19921875 to 0.19921875
- row_counts: int32 [128], replicated, may hold values from 32 to 128, as said below
- log_temp: float32 [1], replicated, may hold values from 3 to 4.1
- bias: float32 [1], replicated, may hold values from -10 to -6
Outputs:
- loss: float32 [1], replicated
- grad_log_temp: float32 [1], replicated
- grad_bias: float32 [1], replicated
- grad_images: float32 [16384, 1152], P(('blk', 'sub'))
- grad_texts: float32 [16384, 1152], P(('blk', 'sub'))
Inputs may be any that keep to these rules, and one draw needn't show every extreme that they name: `row_counts`: each count is a multiple of 32; some member holds exactly 128.
All inputs are finite; a program needn't handle non-finite values.
Results may differ from a plain program's by a relative error of at most 0.0035.
The roundings to bfloat16 on the way count: a program that leaves them out, or rounds other values in their place, can miss the bound.
Values may be sent and summed in bfloat16 or wider, within the bound.
A program may use at most 64 MiB of HBM per device.

v0:
```python
import jax
import jax.numpy as jnp
from jax import lax
from jax.sharding import PartitionSpec as P


def from_partner(value, axis, bit):
    mask = 2**bit
    pairs = [(source, source ^ mask) for source in range(lax.axis_size(axis))]
    return lax.ppermute(value, axis, pairs)


def as_sent(value):

    def short(part):
        return part.astype(jnp.bfloat16) if part.dtype == jnp.float32 else part

    return jax.tree.map(short, value)


def passed_along(value, axis, steps):
    count = lax.axis_size(axis)
    pairs = [(source, (source + steps) % count) for source in range(count)]
    return lax.ppermute(value, axis, pairs)


def normalize(values):
    wide = values.astype(jnp.float32)
    length = jnp.sqrt(jnp.sum(wide * wide, axis=1, keepdims=True) + 1e-06)
    return (wide / length, length)


def project(grad, unit, length):
    return (grad - unit * jnp.sum(unit * grad, axis=1, keepdims=True)) / length


def pair_terms(block, live, piece, col_global, col_used, img_global, temp, shift):
    logits = (
        temp
        * lax.dot_general(
            block, piece, (((1,), (1,)), ((), ())), preferred_element_type=jnp.float32
        )
        + shift
    )
    sign = jnp.where(img_global[:, None] == col_global[None, :], 1.0, -1.0)
    mask = live[:, None] & col_used[None, :]
    pair = jnp.where(mask, jax.nn.softplus(-sign * logits), 0.0)
    slope = jnp.where(mask, -sign * jax.nn.sigmoid(-sign * logits), 0.0)
    weight = (slope * temp).astype(jnp.bfloat16)
    txt_term = lax.dot_general(
        weight, block, (((0,), (0,)), ((), ())), preferred_element_type=jnp.float32
    )
    sums = jnp.stack([jnp.sum(pair), jnp.sum(slope), jnp.sum(slope * (logits - shift))])
    return (weight, txt_term, sums)


def body(images, texts, row_counts, log_temp, bias):
    member = lax.axis_index("blk")
    quarter_idx = lax.axis_index("sub")
    members_all = lax.axis_size("blk")
    quarter = texts.shape[0]
    capacity = quarter * lax.axis_size("sub")
    width = images.shape[1]
    temp = jnp.exp(log_temp[0])
    shift = bias[0]
    img_unit, img_length = normalize(images)
    txt_unit, txt_length = normalize(texts)
    own_block = lax.all_gather(img_unit.astype(jnp.bfloat16), "sub", axis=0, tiled=True)
    partner = from_partner(own_block, "blk", 0)
    odd = jnp.mod(member, 2) == 1
    pair_block = jnp.where(
        odd,
        jnp.concatenate([partner, own_block], axis=0),
        jnp.concatenate([own_block, partner], axis=0),
    )
    stride = 2
    base = member - jnp.mod(member, stride)
    block_slots = jnp.arange(stride * capacity, dtype=jnp.int32)
    img_members = base + block_slots // capacity
    img_global = base * capacity + block_slots
    live = jnp.mod(block_slots, capacity) < jnp.take(row_counts, img_members)
    txt_half = txt_unit.astype(jnp.bfloat16)
    steps_all = members_all // stride
    inner = 4
    groups = steps_all // inner

    def visit(position, lanes, pieces, grads, sums):
        col_global = []
        col_used = []
        for lane, piece in zip(lanes, pieces):
            source = jnp.mod(member - lane[2] * stride * position, members_all)
            local = quarter_idx * quarter + lane[1] + jnp.arange(piece.shape[0], dtype=jnp.int32)
            col_global.append(source * capacity + local)
            col_used.append(local < row_counts[source])
        joined = jnp.concatenate(list(pieces), axis=0)
        glob_all = jnp.concatenate(col_global, axis=0)
        used_all = jnp.concatenate(col_used, axis=0)
        weight, txt_term, part_sums = pair_terms(
            pair_block, live, joined, glob_all, used_all, img_global, temp, shift
        )
        fresh = []
        start = 0
        for piece, txt_acc in zip(pieces, grads):
            count = piece.shape[0]
            fresh.append(txt_acc + txt_term[start : start + count])
            start = start + count
        return (weight, joined, tuple(fresh), sums + part_sums)

    def circulate(lanes, img_acc, sums):
        pieces = tuple((lane[0] for lane in lanes))
        grads = tuple((jnp.zeros(lane[0].shape, jnp.float32) for lane in lanes))

        def run_group(group, carry, last):
            pieces, grads, img_acc, sums = carry
            weights = []
            stacked = []
            for step in range(inner):
                position = group * inner + step
                weight, joined, grads, sums = visit(position, lanes, pieces, grads, sums)
                weights.append(weight)
                stacked.append(joined)
                if not (last and step == inner - 1):
                    pieces = tuple((lane[3](piece) for lane, piece in zip(lanes, pieces)))
                grads = tuple((lane[4](grad) for lane, grad in zip(lanes, grads)))
            img_acc = img_acc + jnp.dot(
                jnp.concatenate(weights, axis=1),
                jnp.concatenate(stacked, axis=0),
                preferred_element_type=jnp.float32,
            )
            return (pieces, grads, img_acc, sums)

        def turn(group, carry):
            return run_group(group, carry, False)

        carry = lax.fori_loop(0, groups - 1, turn, (pieces, grads, img_acc, sums))
        pieces, grads, img_acc, sums = run_group(groups - 1, carry, True)
        return (grads, img_acc, sums)

    img_acc = jnp.zeros((stride * capacity, width), jnp.float32)
    sums = jnp.zeros((3,), jnp.float32)

    def text_onward(piece):
        return jax.tree.map(
            lambda part, own: part.astype(own.dtype),
            passed_along(as_sent(piece), "blk", stride),
            piece,
        )

    def grad_onward(grad):
        return passed_along(grad, "blk", stride)

    grads, img_acc, sums = circulate([(txt_half, 0, 1, text_onward, grad_onward)], img_acc, sums)
    txt_dir = grads[0]
    first_rows = img_acc[:capacity]
    second_rows = img_acc[capacity:]
    mine = jnp.where(odd, second_rows, first_rows)
    theirs = jnp.where(odd, first_rows, second_rows)
    received = from_partner(theirs, "blk", 0)
    img_dir = lax.psum_scatter(mine + received, "sub", scatter_dimension=0, tiled=True)
    totals = lax.psum(sums, ("blk", "sub"))
    used = jnp.sum(row_counts).astype(jnp.float32)
    loss = totals[0:1] / used
    grad_log_temp = totals[2:3] / used
    grad_bias = totals[1:2] / used
    return (
        loss,
        grad_log_temp,
        grad_bias,
        project(img_dir, img_unit, img_length),
        project(txt_dir, txt_unit, txt_length),
    )


def solution(mesh):
    return jax.shard_map(
        body,
        mesh=mesh,
        in_specs=(P(("blk", "sub"), None), P(("blk", "sub"), None), P(), P(), P()),
        out_specs=(P(), P(), P(), P(("blk", "sub"), None), P(("blk", "sub"), None)),
        check_vma=False,
    )
```

profile of v0, /device:TPU:1, one launch (start us, length us, event | category | flops | bytes accessed | tf_op | source)
XLA Modules:
  0.0 1903.7 jit_solution(14205174756315418626)
XLA Ops:
  9.2 15.6 all_gather.3
  41.4 1523.7 %while.22 = (s32[]{:T(128)}, bf16[32,1152]{1,0:T(8,128)(2,1)S(1)}, f32[32,1152]{1,0:T(8,128)S(1)}, f32[256,1152]{1,0:T(8,128)S(1)}, f32[3]{0:T(128)S(1)}, /*inde...) while((s32[]{:T(128)}, bf16[32,1152]{1,0:T(8,128)(2,1)S(1)}, ...), condition=%wide.region_15.16_spmd.clone, body=%wide.region_2.15_spmd.clone.sunk | while | flops 229524192 | bytes 13784080 | solution.py:135
  101.8 12.1 collective-permute-done.5
  116.0 11.9 collective-permute-done.6
  201.8 15.8 collective-permute-done.5
  219.7 14.0 collective-permute-done.6
  308.7 12.9 collective-permute-done.5
  323.8 11.9 collective-permute-done.6
  379.0 12.1 collective-permute-done.2
  409.5 12.5 collective-permute-done.5
  424.1 13.1 collective-permute-done.6
  467.8 11.2 collective-permute-done.1
  481.8 11.1 collective-permute-done.2
  511.5 11.9 collective-permute-done.5
  525.5 11.9 collective-permute-done.6
  569.8 11.6 collective-permute-done.1
  584.2 11.2 collective-permute-done.2
  614.2 13.2 collective-permute-done.5
  629.5 13.3 collective-permute-done.6
  716.6 11.9 collective-permute-done.5
  730.6 11.9 collective-permute-done.6
  774.3 11.4 collective-permute-done.1
  818.6 11.9 collective-permute-done.5
  832.7 12.1 collective-permute-done.6
  918.5 12.3 collective-permute-done.5
  932.9 12.6 collective-permute-done.6
  976.5 11.5 collective-permute-done.1
  1019.5 13.4 collective-permute-done.5
  1035.0 13.1 collective-permute-done.6
  1121.1 13.0 collective-permute-done.5
  1136.2 12.7 collective-permute-done.6
  1221.5 12.5 collective-permute-done.5
  1236.1 11.9 collective-permute-done.6
  1291.8 11.2 collective-permute-done.2
  1322.6 12.1 collective-permute-done.5
  1336.9 11.9 collective-permute-done.6
  1380.1 11.4 collective-permute-done.1
  1394.3 11.2 collective-permute-done.2
  1423.8 12.5 collective-permute-done.5
  1438.5 12.7 collective-permute-done.6
  1511.2 11.2 collective-permute-done.4
  1524.8 12.2 collective-permute-done.5
  1539.2 11.9 collective-permute-done.6
  1567.3 12.5 collective-permute-done.9
  1582.0 11.0 collective-permute-done.10
  1610.8 128.4 %collective-permute-start.12 = (f32[128,1152]{1,0:T(8,128)}, f32[128,1152]{1,0:T(8,128)S(1)}, u32[]{:S(2)}, u32[]{:S(2)}) collective-permute-start(f32[128,1152]{1,0:T(8,128)} %slice_select_fusion), channel_id=1, source_target_pairs={{0,4},{4,0},{8,12},{12,8},{16,20},{20,16},{24,28},{28,24},{32,36},... | collective-permute-start | bytes 1769480 | tf_op jit(solution)/shard_map/ppermute | solution.py:10
  1742.1 12.2 collective-permute-done.14
  1778.5 108.6 %psum.7 = f32[3]{0:T(128)S(1)} all-reduce(f32[3]{0:T(128)S(1)} %maximum_add_fusion.2), channel_id=1, replica_groups=mesh['blk'=128,'sub'=4] {'blk','sub'}, use_global_device_ids=true, to_apply=%region_28.29 | all-reduce | flops 3 | bytes 24 | tf_op jit(solution)/shard_map/psum | solution.py:160
  (655 shorter events, 1087.1 us)
Async XLA Ops:
  7.2 1883.5 %reduce-scatter.2.cloned.1.call-start = ((), (), s32[]{:S(2)}) async-start(), calls=%async_computation.1 | async-start | bytes 737280 | tf_op jit(solution)/shard_map/reduce_scatter | solution.py:159
  24.9 16.4 collective-permute-start.8
  84.5 15.0 collective-permute-start.4
  86.4 51.0 %collective-permute-start.3 = (bf16[32,1152]{1,0:T(8,128)(2,1)S(1)}, bf16[32,1152]{1,0:T(8,128)(2,1)S(1)}, u32[]{:S(2)}, u32[]{:S(2)}) collective-permute-start(bf16[32,1152]{1,0:T(8,128)(2,1)S(1)} %collective-permute-done.2), channel_id=1, source_target_pairs={{0,8},{4,12},{8,16},{12,20},{16,24},{20,28},{24,32},{28,36},{32,40... | collective-permute-start | bytes 221192 | tf_op jit(solution)/shard_map/while/body/eval_jaxpr/ppermute | solution.py:24
  127.9 14.8 collective-permute-start.7
  184.3 15.1 collective-permute-start.4
  186.2 57.0 %collective-permute-start.3 = (bf16[32,1152]{1,0:T(8,128)(2,1)S(1)}, bf16[32,1152]{1,0:T(8,128)(2,1)S(1)}, u32[]{:S(2)}, u32[]{:S(2)}) collective-permute-start(bf16[32,1152]{1,0:T(8,128)(2,1)S(1)} %collective-permute-done.2), channel_id=1, source_target_pairs={{0,8},{4,12},{8,16},{12,20},{16,24},{20,28},{24,32},{28,36},{32,40... | collective-permute-start | bytes 221192 | tf_op jit(solution)/shard_map/while/body/eval_jaxpr/ppermute | solution.py:24
  199.6 18.0 collective-permute-start.5
  217.6 16.2 collective-permute-start.6
  233.8 15.0 collective-permute-start.7
  291.4 15.0 collective-permute-start.4
  293.3 51.9 %collective-permute-start.3 = (bf16[32,1152]{1,0:T(8,128)(2,1)S(1)}, bf16[32,1152]{1,0:T(8,128)(2,1)S(1)}, u32[]{:S(2)}, u32[]{:S(2)}) collective-permute-start(bf16[32,1152]{1,0:T(8,128)(2,1)S(1)} %collective-permute-done.2), channel_id=1, source_target_pairs={{0,8},{4,12},{8,16},{12,20},{16,24},{20,28},{24,32},{28,36},{32,40... | collective-permute-start | bytes 221192 | tf_op jit(solution)/shard_map/while/body/eval_jaxpr/ppermute | solution.py:24
  306.6 15.1 collective-permute-start.5
  376.2 15.0 collective-permute-start.2
  395.0 51.6 %collective-permute-start.3 = (bf16[32,1152]{1,0:T(8,128)(2,1)S(1)}, bf16[32,1152]{1,0:T(8,128)(2,1)S(1)}, u32[]{:S(2)}, u32[]{:S(2)}) collective-permute-start(bf16[32,1152]{1,0:T(8,128)(2,1)S(1)} %collective-permute-done.2), channel_id=1, source_target_pairs={{0,8},{4,12},{8,16},{12,20},{16,24},{20,28},{24,32},{28,36},{32,40... | collective-permute-start | bytes 221192 | tf_op jit(solution)/shard_map/while/body/eval_jaxpr/ppermute | solution.py:24
  422.0 15.2 collective-permute-start.6
  496.8 50.0 %collective-permute-start.3 = (bf16[32,1152]{1,0:T(8,128)(2,1)S(1)}, bf16[32,1152]{1,0:T(8,128)(2,1)S(1)}, u32[]{:S(2)}, u32[]{:S(2)}) collective-permute-start(bf16[32,1152]{1,0:T(8,128)(2,1)S(1)} %collective-permute-done.2), channel_id=1, source_target_pairs={{0,8},{4,12},{8,16},{12,20},{16,24},{20,28},{24,32},{28,36},{32,40... | collective-permute-start | bytes 221192 | tf_op jit(solution)/shard_map/while/body/eval_jaxpr/ppermute | solution.py:24
  537.5 15.0 collective-permute-start.7
  599.3 53.0 %collective-permute-start.3 = (bf16[32,1152]{1,0:T(8,128)(2,1)S(1)}, bf16[32,1152]{1,0:T(8,128)(2,1)S(1)}, u32[]{:S(2)}, u32[]{:S(2)}) collective-permute-start(bf16[32,1152]{1,0:T(8,128)(2,1)S(1)} %collective-permute-done.2), channel_id=1, source_target_pairs={{0,8},{4,12},{8,16},{12,20},{16,24},{20,28},{24,32},{28,36},{32,40... | collective-permute-start | bytes 221192 | tf_op jit(solution)/shard_map/while/body/eval_jaxpr/ppermute | solution.py:24
  612.0 15.3 collective-permute-start.5
  627.4 15.5 collective-permute-start.6
  642.9 14.8 collective-permute-start.7
  702.1 49.8 %collective-permute-start.3 = (bf16[32,1152]{1,0:T(8,128)(2,1)S(1)}, bf16[32,1152]{1,0:T(8,128)(2,1)S(1)}, u32[]{:S(2)}, u32[]{:S(2)}) collective-permute-start(bf16[32,1152]{1,0:T(8,128)(2,1)S(1)} %collective-permute-done.2), channel_id=1, source_target_pairs={{0,8},{4,12},{8,16},{12,20},{16,24},{20,28},{24,32},{28,36},{32,40... | collective-permute-start | bytes 221192 | tf_op jit(solution)/shard_map/while/body/eval_jaxpr/ppermute | solution.py:24
  742.5 15.7 collective-permute-start.7
  800.9 15.4 collective-permute-start.4
  802.8 51.4 %collective-permute-start.3 = (bf16[32,1152]{1,0:T(8,128)(2,1)S(1)}, bf16[32,1152]{1,0:T(8,128)(2,1)S(1)}, u32[]{:S(2)}, u32[]{:S(2)}) collective-permute-start(bf16[32,1152]{1,0:T(8,128)(2,1)S(1)} %collective-permute-done.2), channel_id=1, source_target_pairs={{0,8},{4,12},{8,16},{12,20},{16,24},{20,28},{24,32},{28,36},{32,40... | collective-permute-start | bytes 221192 | tf_op jit(solution)/shard_map/while/body/eval_jaxpr/ppermute | solution.py:24
  844.8 15.2 collective-permute-start.7
  903.8 51.1 %collective-permute-start.3 = (bf16[32,1152]{1,0:T(8,128)(2,1)S(1)}, bf16[32,1152]{1,0:T(8,128)(2,1)S(1)}, u32[]{:S(2)}, u32[]{:S(2)}) collective-permute-start(bf16[32,1152]{1,0:T(8,128)(2,1)S(1)} %collective-permute-done.2), channel_id=1, source_target_pairs={{0,8},{4,12},{8,16},{12,20},{16,24},{20,28},{24,32},{28,36},{32,40... | collective-permute-start | bytes 221192 | tf_op jit(solution)/shard_map/while/body/eval_jaxpr/ppermute | solution.py:24
  930.7 14.7 collective-permute-start.6
  945.5 15.0 collective-permute-start.7
  1005.1 52.5 %collective-permute-start.3 = (bf16[32,1152]{1,0:T(8,128)(2,1)S(1)}, bf16[32,1152]{1,0:T(8,128)(2,1)S(1)}, u32[]{:S(2)}, u32[]{:S(2)}) collective-permute-start(bf16[32,1152]{1,0:T(8,128)(2,1)S(1)} %collective-permute-done.2), channel_id=1, source_target_pairs={{0,8},{4,12},{8,16},{12,20},{16,24},{20,28},{24,32},{28,36},{32,40... | collective-permute-start | bytes 221192 | tf_op jit(solution)/shard_map/while/body/eval_jaxpr/ppermute | solution.py:24
  1017.4 15.5 collective-permute-start.5
  1032.9 15.2 collective-permute-start.6
  1106.5 51.8 %collective-permute-start.3 = (bf16[32,1152]{1,0:T(8,128)(2,1)S(1)}, bf16[32,1152]{1,0:T(8,128)(2,1)S(1)}, u32[]{:S(2)}, u32[]{:S(2)}) collective-permute-start(bf16[32,1152]{1,0:T(8,128)(2,1)S(1)} %collective-permute-done.2), channel_id=1, source_target_pairs={{0,8},{4,12},{8,16},{12,20},{16,24},{20,28},{24,32},{28,36},{32,40... | collective-permute-start | bytes 221192 | tf_op jit(solution)/shard_map/while/body/eval_jaxpr/ppermute | solution.py:24
  1119.0 15.1 collective-permute-start.5
  1134.1 14.8 collective-permute-start.6
  1207.1 50.4 %collective-permute-start.3 = (bf16[32,1152]{1,0:T(8,128)(2,1)S(1)}, bf16[32,1152]{1,0:T(8,128)(2,1)S(1)}, u32[]{:S(2)}, u32[]{:S(2)}) collective-permute-start(bf16[32,1152]{1,0:T(8,128)(2,1)S(1)} %collective-permute-done.2), channel_id=1, source_target_pairs={{0,8},{4,12},{8,16},{12,20},{16,24},{20,28},{24,32},{28,36},{32,40... | collective-permute-start | bytes 221192 | tf_op jit(solution)/shard_map/while/body/eval_jaxpr/ppermute | solution.py:24
  1305.0 15.3 collective-permute-start.4
  1306.9 51.3 %collective-permute-start.3 = (bf16[32,1152]{1,0:T(8,128)(2,1)S(1)}, bf16[32,1152]{1,0:T(8,128)(2,1)S(1)}, u32[]{:S(2)}, u32[]{:S(2)}) collective-permute-start(bf16[32,1152]{1,0:T(8,128)(2,1)S(1)} %collective-permute-done.2), channel_id=1, source_target_pairs={{0,8},{4,12},{8,16},{12,20},{16,24},{20,28},{24,32},{28,36},{32,40... | collective-permute-start | bytes 221192 | tf_op jit(solution)/shard_map/while/body/eval_jaxpr/ppermute | solution.py:24
  1348.8 15.3 collective-permute-start.7
  1409.4 51.2 %collective-permute-start.3 = (bf16[32,1152]{1,0:T(8,128)(2,1)S(1)}, bf16[32,1152]{1,0:T(8,128)(2,1)S(1)}, u32[]{:S(2)}, u32[]{:S(2)}) collective-permute-start(bf16[32,1152]{1,0:T(8,128)(2,1)S(1)} %collective-permute-done.2), channel_id=1, source_target_pairs={{0,8},{4,12},{8,16},{12,20},{16,24},{20,28},{24,32},{28,36},{32,40... | collective-permute-start | bytes 221192 | tf_op jit(solution)/shard_map/while/body/eval_jaxpr/ppermute | solution.py:24
  1436.4 14.8 collective-permute-start.6
  1506.8 15.6 collective-permute-start.4
  1508.8 51.7 %collective-permute-start.3 = (bf16[32,1152]{1,0:T(8,128)(2,1)S(1)}, bf16[32,1152]{1,0:T(8,128)(2,1)S(1)}, u32[]{:S(2)}, u32[]{:S(2)}) collective-permute-start(bf16[32,1152]{1,0:T(8,128)(2,1)S(1)} %collective-permute-done.2), channel_id=1, source_target_pairs={{0,8},{4,12},{8,16},{12,20},{16,24},{20,28},{24,32},{28,36},{32,40... | collective-permute-start | bytes 221192 | tf_op jit(solution)/shard_map/while/body/eval_jaxpr/ppermute | solution.py:24
  1565.1 14.7 collective-permute-start.9
  1607.6 132.2 %collective-permute-start.13 = (f32[32,1152]{1,0:T(8,128)S(1)}, f32[32,1152]{1,0:T(8,128)S(1)}, u32[]{:S(2)}, u32[]{:S(2)}) collective-permute-start(f32[32,1152]{1,0:T(8,128)S(1)} %convolution_add_fusion.5), channel_id=1, source_target_pairs={{0,8},{4,12},{8,16},{12,20},{16,24},{20,28},{24,32},{28,36},{32,40... | collective-permute-start | bytes 442376 | tf_op jit(solution)/shard_map/ppermute | solution.py:24
  1610.8 145.5 %collective-permute-start.12 = (f32[128,1152]{1,0:T(8,128)}, f32[128,1152]{1,0:T(8,128)S(1)}, u32[]{:S(2)}, u32[]{:S(2)}) collective-permute-start(f32[128,1152]{1,0:T(8,128)} %slice_select_fusion), channel_id=1, source_target_pairs={{0,4},{4,0},{8,12},{12,8},{16,20},{20,16},{24,28},{28,24},{32,36},... | collective-permute-start | bytes 1769480 | tf_op jit(solution)/shard_map/ppermute | solution.py:10
  1768.4 121.3 %collective-permute-start.16 = (f32[32,1152]{1,0:T(8,128)S(1)}, f32[32,1152]{1,0:T(8,128)S(1)}, u32[]{:S(2)}, u32[]{:S(2)}) collective-permute-start(f32[32,1152]{1,0:T(8,128)S(1)} %add.840), channel_id=1, source_target_pairs={{0,8},{4,12},{8,16},{12,20},{16,24},{20,28},{24,32},{28,36},{32,40... | collective-permute-start | bytes 442376 | tf_op jit(solution)/shard_map/ppermute | solution.py:24
  (107 other events, 12738.5 us)
Sparse Core Ops, SparseCore 0:
  1757.4 36.1 reduce-scatter.1
where the time goes:
time: 1910 us; the launch traced here: 1900 us
  waiting for transfers between devices  1100 us (58%)
  starting transfers between devices  380 us (20%)
  other arithmetic  172 us (9%)
  blocking collectives  124 us (6%)
  matrix products  89.1 us (5%)
  between operations  22 us (1%)
    ppermute x127, waiting for transfers between devices, passed_along(): return lax.ppermute(value, axis, pairs)  1100 us
    ppermute x127, starting transfers between devices, passed_along(): return lax.ppermute(value, axis, pairs)  244 us
    ppermute x2, starting transfers between devices, from_partner(): return lax.ppermute(value, axis, pairs)  136 us
    add x16, other arithmetic, visit(): return (weight, joined, tuple(fresh), sums + part_sums)  120 us
    psum x1, blocking collectives, body(): totals = lax.psum(sums, ('blk', 'sub'))  109 us
    dot_general x64, matrix products, pair_terms(): lax.dot_general(block, piece, (((1,), (1,)), ((), ())), preferred_element...  67.7 us
    lt x33, other arithmetic, visit(): col_used.append(local < row_counts[source])  39.1 us
  transfers between devices with their start and end apart: 130, of which 110 were waited for; matrix products, arithmetic and copies ran while one was open for 13% of the time, Pallas kernels for 0%

commit v1 on v0

v1 whole, which is shorter than its diff:
```python
import functools

import jax
import jax.numpy as jnp
from jax import lax
from jax.experimental import pallas as pl
from jax.experimental.pallas import tpu as pltpu
from jax.sharding import PartitionSpec as P

MESH = pl.DeviceIdType.MESH
F32 = jnp.float32
BF16 = jnp.bfloat16
T = 32
RING = 8
NEAR_FIRST = (1, 7, 2, 6, 3, 5, 4)

IMG, TXT, RED_C, RED_XT, RED_Z, RED_XI, RED_Y, SCAL = 0, 16, 48, 64, 72, 80, 88, 96
N_SEM = 120


def place():
    blk, sub = lax.axis_index("blk"), lax.axis_index("sub")
    core = lax.rem(blk, 2)
    y = lax.rem(lax.div(blk, 2), RING)
    z = lax.rem(lax.div(blk, 16), 2) * 4 + sub
    x = lax.div(blk, 32)
    return x, y, z, core


def member(x, y, z, core):
    return ((x * 2 + lax.div(z, 4)) * RING + y) * 2 + core


def device(x, y, z, core):
    return (member(x, y, z, core), lax.rem(z, 4))


def ring(value):
    return lax.rem(value, RING)


def normalized(values):
    wide = values.astype(F32)
    length = jnp.sqrt(jnp.sum(wide * wide, axis=1, keepdims=True) + 1e-06)
    return wide / length, length


def projected(grad, unit, length):
    return (grad - unit * jnp.sum(unit * grad, axis=1, keepdims=True)) / length


def sigmoid_and_softplus(u):
    small = jnp.exp(-jnp.abs(u))
    ratio = 1.0 / (1.0 + small)
    sigmoid = jnp.where(u >= 0.0, ratio, small * ratio)
    softplus = jnp.maximum(u, 0.0) + jnp.log1p(small)
    return sigmoid, softplus


def tile(slot):
    return pl.ds(slot * T, T)


def kernel(
    img_in, txt_in, counts, counts_row, log_temp, bias,
    loss, grad_log_temp, grad_bias, grad_img, grad_txt,
    img, txt, weight, logits, txt_part, img_part, part_a, part_b, part_i,
    from_c, from_xt, from_z, from_xi, from_y, scal, ssem, rsem,
):
    x, y, z, core = place()
    pair_i = x + 1 - 2 * lax.rem(x, 2)
    pair_t = lax.rem(x + 3 + 2 * lax.rem(x, 2), 4)

    def y_peer(d):
        return device(x, ring(y + d), z, core)

    def z_peer(d):
        return device(x, y, ring(z + d), core)

    my_xc = x * 2 + core

    def xc_peer(d):
        other = ring(my_xc + d)
        return device(lax.div(other, 2), y, z, lax.rem(other, 2))

    img_mate = device(pair_i, y, z, core)
    txt_mate = device(pair_t, y, z, core)
    core_mate = device(x, y, z, 1 - core)

    barrier = pltpu.get_barrier_semaphore()
    for d in range(1, RING):
        for peer in (y_peer(d), z_peer(d), xc_peer(d)):
            pl.semaphore_signal(barrier, inc=1, device_id=peer, device_id_type=MESH)

    temp = jnp.exp(jnp.full((1, 1), log_temp[0], F32))
    shift = bias[0]
    img_unit, img_length = normalized(img_in[...])
    txt_unit, txt_length = normalized(txt_in[...])

    def tile_used(x, y, z, core):
        return jnp.where(counts[member(x, y, z, core)] > T * lax.rem(z, 4), 1.0, 0.0)

    own_used = tile_used(x, y, z, core)
    img_half = jnp.where(own_used > 0.0, img_unit, 0.0).astype(BF16)
    txt_half = jnp.where(own_used > 0.0, txt_unit, 0.0).astype(BF16)
    img[tile(0), :] = img_half
    txt[tile(0), :] = txt_half

    def copy(src, dst, index, peer):
        return pltpu.make_async_remote_copy(
            src_ref=src,
            dst_ref=dst,
            send_sem=ssem.at[index],
            recv_sem=rsem.at[index],
            device_id=peer,
            device_id_type=MESH,
        )

    sent = []

    def start(made):
        made.start()
        sent.append(made)
        return made

    pl.semaphore_wait(barrier, 3 * (RING - 1))

    img_got, txt_got = {}, {}
    for s in NEAR_FIRST:
        txt_got[s] = start(copy(txt.at[tile(0)], txt.at[tile(s)], TXT + s, z_peer(RING - s)))
        img_got[s] = start(copy(img.at[tile(0)], img.at[tile(s)], IMG + s, y_peer(RING - s)))

    def pass_on(s):
        txt_got[8 + s] = start(copy(txt.at[tile(s)], txt.at[tile(8 + s)], TXT + 8 + s, txt_mate))
        img_got[8 + s] = start(copy(img.at[tile(s)], img.at[tile(8 + s)], IMG + 8 + s, img_mate))
        txt_got[16 + s] = start(copy(txt.at[tile(s)], txt.at[tile(16 + s)], TXT + 16 + s, core_mate))

    pass_on(0)

    img_wide, txt_wide = img_half.astype(F32), txt_half.astype(F32)
    own_u = temp * jnp.sum(img_wide * txt_wide, axis=1, keepdims=True) + shift
    own_sigmoid, own_softplus = sigmoid_and_softplus(-own_u)
    own_slope = -own_sigmoid * own_used
    own_pair = own_softplus * own_used
    own_weight = (own_slope * temp).astype(BF16).astype(F32)
    own_sums = (jnp.sum(own_pair), jnp.sum(own_slope), jnp.sum(own_slope * (own_u - shift)))

    for s in NEAR_FIRST:
        txt_got[s].wait_recv()
        img_got[s].wait_recv()
        pass_on(s)
    for s in (0, *NEAR_FIRST):
        txt_got[8 + s].wait_recv()
        txt_got[24 + s] = start(copy(txt.at[tile(8 + s)], txt.at[tile(24 + s)], TXT + 24 + s, core_mate))
    for s in (0, *NEAR_FIRST):
        img_got[8 + s].wait_recv()
        txt_got[16 + s].wait_recv()
        txt_got[24 + s].wait_recv()

    def block(c, sums):
        rows = pl.ds(pl.multiple_of(c * 256, 256), 256)
        logits[...] = lax.dot_general(
            txt[rows, :], img[...], (((1,), (1,)), ((), ())), preferred_element_type=F32
        )
        tx = jnp.where(lax.rem(c, 2) == 1, pair_t, x)
        tc = jnp.where(c >= 2, 1 - core, core)
        pair_sum, slope_sum, scaled_sum = sums
        for k in range(8):
            scaled = logits[tile(k), :] * temp
            u = scaled + shift
            slope, pair = sigmoid_and_softplus(u)
            if k == 0:
                row = lax.broadcasted_iota(jnp.int32, (T, 512), 0)
                column = lax.broadcasted_iota(jnp.int32, (T, 512), 1)
                own = (row == column) & (c == 0)
                slope = jnp.where(own, 0.0, slope)
                pair = jnp.where(own, 0.0, pair)
            weight[pl.ds(pl.multiple_of(c * 256 + k * T, T), T), :] = (slope * temp).astype(BF16)
            used = tile_used(tx, y, ring(z + k), tc)

            def folded(value):
                return jnp.sum(value.reshape(T // 8, 8, 512), axis=0)

            pair_sum = pair_sum + used * folded(pair)
            slope_sum = slope_sum + used * folded(slope)
            scaled_sum = scaled_sum + folded(slope * scaled)
        return pair_sum, slope_sum, scaled_sum

    zero = jnp.zeros((8, 512), F32)
    pair_sum, slope_sum, scaled_sum = lax.fori_loop(0, 4, block, (zero, zero, zero))

    column_tile = lax.broadcasted_iota(jnp.int32, (8, 512), 1) // T
    columns_used = zero
    for s in range(16):
        used = tile_used(x if s < 8 else pair_i, ring(y + s), z, core)
        columns_used = jnp.where(column_tile == s, used, columns_used)
    sums = (
        jnp.sum(pair_sum * columns_used) + own_sums[0],
        jnp.sum(slope_sum * columns_used) + own_sums[1],
        jnp.sum(scaled_sum) + own_sums[2],
    )
    lane = lax.broadcasted_iota(jnp.int32, (8, 128), 1)
    vector = jnp.where(lane == 0, sums[0], jnp.where(lane == 1, sums[1], jnp.where(lane == 2, sums[2], 0.0)))

    def spread(stage, mine, peer_of, value):
        scal[stage, mine] = value
        for d in range(1, RING):
            index = SCAL + stage * 8 + mine
            made = pltpu.make_async_remote_copy(
                src_ref=scal.at[stage, mine],
                dst_ref=scal.at[stage, mine],
                send_sem=ssem.at[SCAL + stage * 8 + d],
                recv_sem=rsem.at[index],
                device_id=peer_of(d),
                device_id_type=MESH,
            )
            start(made)

    def summed(stage, mine, peer_of):
        for d in range(1, RING):
            other = ring(mine + d)
            pltpu.make_async_remote_copy(
                src_ref=scal.at[stage, mine],
                dst_ref=scal.at[stage, other],
                send_sem=ssem.at[SCAL + stage * 8 + d],
                recv_sem=rsem.at[SCAL + stage * 8 + other],
                device_id=peer_of(d),
                device_id_type=MESH,
            ).wait_recv()
        total = scal[stage, 0]
        for k in range(1, RING):
            total = total + scal[stage, k]
        return total

    spread(0, y, y_peer, vector)

    def image_dir(first):
        return lax.dot_general(
            weight[:, first : first + 256], txt[...], (((0,), (0,)), ((), ())), preferred_element_type=F32
        )

    def text_dir(first):
        return jnp.dot(weight[first : first + 256, :], img[...], preferred_element_type=F32)

    img_part[256:512, :] = image_dir(256).astype(BF16)
    xi = {}
    for s in range(8):
        xi[s] = start(copy(img_part.at[tile(8 + s)], from_xi.at[tile(s)], RED_XI + s, img_mate))

    txt_part[768:1024, :] = text_dir(768).astype(BF16)
    c_d = start(copy(txt_part.at[pl.ds(768, 256)], from_c.at[pl.ds(256, 256)], RED_C + 1, core_mate))
    part_b[...] = text_dir(256)

    total = summed(0, y, y_peer)
    spread(1, z, z_peer, total)

    c_d.wait_recv()
    xt = {}
    for s in range(8):
        both = part_b[tile(s), :] + from_c[tile(8 + s), :].astype(F32)
        txt_part[tile(8 + s), :] = both.astype(BF16)
        xt[s] = start(copy(txt_part.at[tile(8 + s)], from_xt.at[tile(s)], RED_XT + s, txt_mate))

    txt_part[512:768, :] = text_dir(512).astype(BF16)
    c_c = start(copy(txt_part.at[pl.ds(512, 256)], from_c.at[pl.ds(0, 256)], RED_C, core_mate))
    part_i[...] = image_dir(0)
    part_a[...] = text_dir(0)

    total = summed(1, z, z_peer)
    spread(2, my_xc, xc_peer, total)

    got_y, got_z = {}, {}
    c_c.wait_recv()
    order = (4, 3, 5, 2, 6, 1, 7, 0)
    for s in order:
        xi[s].wait_recv()
        both = part_i[tile(s), :] + from_xi[tile(s), :].astype(F32)
        if s == 0:
            img_dir = both
        else:
            img_part[tile(s), :] = both.astype(BF16)
            got_y[RING - s] = start(copy(img_part.at[tile(s)], from_y.at[tile(RING - s)], RED_Y + RING - s, y_peer(s)))
        xt[s].wait_recv()
        both = part_a[tile(s), :] + from_c[tile(s), :].astype(F32) + from_xt[tile(s), :].astype(F32)
        if s == 0:
            txt_dir = both
        else:
            txt_part[tile(s), :] = both.astype(BF16)
            got_z[RING - s] = start(copy(txt_part.at[tile(s)], from_z.at[tile(RING - s)], RED_Z + RING - s, z_peer(s)))

    total = summed(2, my_xc, xc_peer)
    used = jnp.sum(counts_row[...].astype(F32))
    means = total / used
    loss[0] = means[0, 0]
    grad_bias[0] = means[0, 1]
    grad_log_temp[0] = means[0, 2]

    img_dir = img_dir + own_weight * txt_wide
    txt_dir = txt_dir + own_weight * img_wide
    for s in NEAR_FIRST:
        got_y[s].wait_recv()
        img_dir = img_dir + from_y[tile(s), :].astype(F32)
    img_dir = jnp.where(own_used > 0.0, img_dir, 0.0)
    grad_img[...] = projected(img_dir, img_unit, img_length)
    for s in NEAR_FIRST:
        got_z[s].wait_recv()
        txt_dir = txt_dir + from_z[tile(s), :].astype(F32)
    txt_dir = jnp.where(own_used > 0.0, txt_dir, 0.0)
    grad_txt[...] = projected(txt_dir, txt_unit, txt_length)

    for made in sent:
        made.wait_send()


def body(images, texts, row_counts, log_temp, bias):
    rows, width = images.shape
    scalar = jax.ShapeDtypeStruct((1,), F32)
    grad = jax.ShapeDtypeStruct((rows, width), F32)
    vmem = pl.BlockSpec(memory_space=pltpu.VMEM)
    smem = pl.BlockSpec(memory_space=pltpu.SMEM)
    return pl.pallas_call(
        kernel,
        out_shape=(scalar, scalar, scalar, grad, grad),
        in_specs=[vmem, vmem, smem, vmem, smem, smem],
        out_specs=(smem, smem, smem, vmem, vmem),
        scratch_shapes=[
            pltpu.VMEM((512, width), BF16),
            pltpu.VMEM((1024, width), BF16),
            pltpu.VMEM((1024, 512), BF16),
            pltpu.VMEM((256, 512), F32),
            pltpu.VMEM((1024, width), BF16),
            pltpu.VMEM((512, width), BF16),
            pltpu.VMEM((256, width), F32),
            pltpu.VMEM((256, width), F32),
            pltpu.VMEM((256, width), F32),
            pltpu.VMEM((512, width), BF16),
            pltpu.VMEM((256, width), BF16),
            pltpu.VMEM((256, width), BF16),
            pltpu.VMEM((256, width), BF16),
            pltpu.VMEM((256, width), BF16),
            pltpu.VMEM((3, 8, 8, 128), F32),
            pltpu.SemaphoreType.DMA((N_SEM,)),
            pltpu.SemaphoreType.DMA((N_SEM,)),
        ],
        compiler_params=pltpu.CompilerParams(
            collective_id=0, has_side_effects=True, vmem_limit_bytes=48 << 20
        ),
        cost_estimate=pl.CostEstimate(flops=6 * 512 * 1024 * width, bytes_accessed=4 << 20, transcendentals=1 << 20),
    )(images, texts, row_counts, row_counts.reshape(1, -1), log_temp, bias)


def solution(mesh):
    return jax.shard_map(
        body,
        mesh=mesh,
        in_specs=(P(("blk", "sub"), None), P(("blk", "sub"), None), P(), P(), P()),
        out_specs=(P(), P(), P(), P(("blk", "sub"), None), P(("blk", "sub"), None)),
        check_vma=False,
    )
```

time: 1910 us -> 83.3 us (0.04)
  waiting for transfers between devices: 1100 us -> 0 us
  starting transfers between devices: 380 us -> 0 us
  other arithmetic: 172 us -> 0 us
  blocking collectives: 124 us -> 0 us
  matrix products: 89.1 us -> 0 us
  Pallas kernels: 0 us -> 72.1 us
    ppermute x129 -> x0, waiting for transfers between devices: 1100 us -> none  [the longest x127 1100 us: passed_along(): return lax.ppermute(value, axis, pairs)]
    ppermute x129 -> x0, starting transfers between devices: 380 us -> none  [the longest x127 244 us: passed_along(): return lax.ppermute(value, axis, pairs)]
    add x98 -> x0, other arithmetic: 122 us -> none  [the longest x16 120 us: visit(): return (weight, joined, tuple(fresh), sums + part_sums)]
    psum x1 -> x0, blocking collectives: 109 us -> none  [body(): totals = lax.psum(sums, ('blk', 'sub'))]
    dot_general x144 -> x0, matrix products: 89.1 us -> none  [the longest x64 67.7 us: pair_terms(): lax.dot_general(block, piece, (((1,), (1,)), ((), ())), preferred_element...]
    pallas_call x0 -> x1, Pallas kernels: none -> 72.1 us  [body(): pl.pallas_call(kernel, out_shape=(scalar, scalar, scalar, grad, grad), in...]
    lt x34 -> x0, other arithmetic: 39.1 us -> none  [the longest x33 39.1 us: visit(): col_used.append(local < row_counts[source])]
  transfers between devices with their start and end apart: 130 -> 0, of which waited for: 110 -> 0; matrix products, arithmetic and copies ran while one was open for 13% -> 0% of each run, Pallas kernels for 0% -> 0%
where the time goes in v1:
time: 83.3 us; the launch traced here: 83 us
  Pallas kernels  72.1 us (87%)
  between operations  7.11 us (9%)
  local copies, waits for them, and re-layouts  3.74 us (4%)
    pallas_call x1, Pallas kernels, body(): pl.pallas_call(kernel, out_shape=(scalar, scalar, scalar, grad, grad), in...  72.1 us
    unnamed x8, local copies, waits for them, and re-layouts  3.74 us

profile of v1, /device:TPU:1, one launch (start us, length us, event | category | flops | bytes accessed | tf_op | source)
XLA Modules:
  0.0 83.0 jit_solution(17003729792166784788)
XLA Ops:
  1.9 0.0 copy-start.2
  1.9 0.6 copy-done.2
  2.6 0.0 copy-start
  2.6 0.9 %copy-done = bf16[32,1152]{1,0:T(8,128)(2,1)S(1)} copy-done((bf16[32,1152]{1,0:T(8,128)(2,1)S(1)}, bf16[32,1152]{1,0:T(8,128)(2,1)}, u32[]{:S(2)}) %copy-start) | copy-done | bytes 73752
  3.5 0.0 copy-start.1
  3.5 0.9 %copy-done.1 = bf16[32,1152]{1,0:T(8,128)(2,1)S(1)} copy-done((bf16[32,1152]{1,0:T(8,128)(2,1)S(1)}, bf16[32,1152]{1,0:T(8,128)(2,1)}, u32[]{:S(2)}) %copy-start.1) | copy-done | bytes 73752
  4.3 72.1 %shard_map.92 = (f32[1]{0:T(128)}, f32[1]{0:T(128)}, f32[1]{0:T(128)}, f32[32,1152]{1,0:T(8,128)S(1)}, f32[32,1152]{1,0:T(8,128)S(1)}) custom-call(bf16[32,1152]{1,0:T(8,128)(2,1)S(1)} %copy-done, bf16[32,1152]{1,0:T(8,128)(2,1)S(1)} %copy-done.1, s32[128]{0:T(128)S(1)} %copy-done.2, s32[1,128]{1,0:T(1,128)S(1)} %bitcast.1, f32[1]{0:T(128)S(6)} %copy.15.log_temp, ...), custom_call_target="tpu_custom_call" | custom-call | flops 3623878656 | bytes 4194304 | tf_op jit(solution)/shard_map/pallas_call | solution.py:321
  78.3 0.7 copy.20
  78.9 0.7 copy.21
Async XLA Ops:
  1.9 0.7 copy-start.2
  2.6 0.9 %copy-start = (bf16[32,1152]{1,0:T(8,128)(2,1)S(1)}, bf16[32,1152]{1,0:T(8,128)(2,1)}, u32[]{:S(2)}) copy-start(bf16[32,1152]{1,0:T(8,128)(2,1)} %img_in.1) | copy-start | bytes 221188
  3.5 0.9 %copy-start.1 = (bf16[32,1152]{1,0:T(8,128)(2,1)S(1)}, bf16[32,1152]{1,0:T(8,128)(2,1)}, u32[]{:S(2)}) copy-start(bf16[32,1152]{1,0:T(8,128)(2,1)} %txt_in.1) | copy-start | bytes 221188

commit v2 on v1

v2 whole, which is shorter than its diff:
```python
import functools

import jax
import jax.numpy as jnp
from jax import lax
from jax.experimental import pallas as pl
from jax.experimental.pallas import tpu as pltpu
from jax.sharding import PartitionSpec as P

MESH = pl.DeviceIdType.MESH
F32 = jnp.float32
BF16 = jnp.bfloat16
T = 32
RING = 8
N_SEM = 192
SCAL = 160
H0, H1 = (0, 16), (16, 16)
FULL = (0, T)


def place():
    blk, sub = lax.axis_index("blk"), lax.axis_index("sub")
    core = lax.rem(blk, 2)
    y = lax.rem(lax.div(blk, 2), RING)
    z = lax.rem(lax.div(blk, 16), 2) * 4 + sub
    x = lax.div(blk, 32)
    return x, y, z, core


def member(x, y, z, core):
    return ((x * 2 + lax.div(z, 4)) * RING + y) * 2 + core


def device(x, y, z, core):
    return (member(x, y, z, core), lax.rem(z, 4))


def ring(value):
    return lax.rem(value, RING)


def normalized(values):
    wide = values.astype(F32)
    length = jnp.sqrt(jnp.sum(wide * wide, axis=1, keepdims=True) + 1e-06)
    return wide / length, length


def projected(grad, unit, length):
    return (grad - unit * jnp.sum(unit * grad, axis=1, keepdims=True)) / length


def sigmoid_and_softplus(u):
    small = jnp.exp(-jnp.abs(u))
    ratio = 1.0 / (1.0 + small)
    sigmoid = jnp.where(u >= 0.0, ratio, small * ratio)
    softplus = jnp.maximum(u, 0.0) + jnp.log1p(small)
    return sigmoid, softplus


def at(slot, part=FULL):
    return pl.ds(slot * T + part[0], part[1])


def tile(slot):
    return pl.ds(slot * T, T)


def kernel(
    img_hbm, txt_hbm, counts_hbm, log_temp_hbm, bias_hbm,
    loss, grad_log_temp, grad_bias, grad_img, grad_txt,
    img_in, txt_in, counts, log_temp, bias, img, txt, weight, logits,
    out_c, from_c, img_sum, txt_sum, img_out, txt_out, img_back, txt_back, scal, local, ssem, rsem,
):
    x, y, z, core = place()
    pair_i = x + 1 - 2 * lax.rem(x, 2)
    pair_t = lax.rem(x + 3 + 2 * lax.rem(x, 2), 4)

    def y_peer(d):
        return device(x, ring(y + d), z, core)

    def z_peer(d):
        return device(x, y, ring(z + d), core)

    my_xc = x * 2 + core

    def xc_peer(d):
        other = ring(my_xc + d)
        return device(lax.div(other, 2), y, z, lax.rem(other, 2))

    img_mate = device(pair_i, y, z, core)
    txt_mate = device(pair_t, y, z, core)
    core_mate = device(x, y, z, 1 - core)

    barrier = pltpu.get_barrier_semaphore()
    for d in range(1, RING):
        for peer in (y_peer(d), z_peer(d), xc_peer(d)):
            pl.semaphore_signal(barrier, inc=1, device_id=peer, device_id_type=MESH)

    fetched = [
        pltpu.make_async_copy(source, target, local.at[k])
        for k, (source, target) in enumerate(
            ((counts_hbm, counts), (log_temp_hbm, log_temp), (bias_hbm, bias), (img_hbm, img_in), (txt_hbm, txt_in))
        )
    ]
    for made in fetched:
        made.start()
    for made in fetched:
        made.wait()

    temp = jnp.exp(jnp.full((1, 1), log_temp[0], F32))
    shift = bias[0]
    img_unit, img_length = normalized(img_in[...])
    txt_unit, txt_length = normalized(txt_in[...])

    def tile_used(x, y, z, core):
        return jnp.where(counts[member(x, y, z, core)] > T * lax.rem(z, 4), 1.0, 0.0)

    own_used = tile_used(x, y, z, core)
    img_half = jnp.where(own_used > 0.0, img_unit, 0.0).astype(BF16)
    txt_half = jnp.where(own_used > 0.0, txt_unit, 0.0).astype(BF16)
    img[tile(0), :] = img_half
    txt[tile(0), :] = txt_half

    sent = []

    def send(src, dst, peer):
        index = len(sent)
        made = pltpu.make_async_remote_copy(
            src_ref=src,
            dst_ref=dst,
            send_sem=ssem.at[index],
            recv_sem=rsem.at[index],
            device_id=peer,
            device_id_type=MESH,
        )
        made.start()
        sent.append(made)
        return made

    img_ring = (img, y_peer(1), y_peer(RING - 1), img_mate)
    txt_ring = (txt, z_peer(1), z_peer(RING - 1), txt_mate)
    rings = (txt_ring, img_ring)

    pl.semaphore_wait(barrier, 3 * (RING - 1))

    def across(which, slot, part):
        buf, _, _, mate = which
        return send(buf.at[at(slot, part)], buf.at[at(8 + slot, part)], mate)

    def forward(which, base, k, part):
        buf, plus, minus, _ = which
        return (
            send(buf.at[at(base + (RING - k + 1) % RING, part)], buf.at[at(base + RING - k, part)], plus),
            send(buf.at[at(base + k - 1, part)], buf.at[at(base + k, part)], minus),
        )

    def to_core(slot):
        return send(txt.at[at(slot)], txt.at[at(16 + slot)], core_mate)

    def last_whole(which):
        buf, plus, minus, _ = which
        return (
            send(buf.at[at(5, H0)], buf.at[at(4, H0)], plus),
            send(buf.at[at(3, H1)], buf.at[at(4, H1)], minus),
        )

    odd = lax.rem(core, 2)

    def toward(which):
        _, plus, minus, _ = which
        return (jnp.where(odd == 1, minus[0], plus[0]), jnp.where(odd == 1, minus[1], plus[1]))

    def last_half(which):
        buf = which[0]
        source = jnp.where(odd == 1, 8 + 3, 8 + 5)
        return (send(buf.at[pl.ds(pl.multiple_of(source * T, T), 16)], buf.at[at(12, H0)], toward(which)),)

    first = [across(r, 0, H0) for r in rings]
    whole = [forward(r, 0, 1, FULL) for r in rings]
    second = [{0: across(r, 0, H1)} for r in rings]
    core_got = [to_core(0)]

    img_wide, txt_wide = img_half.astype(F32), txt_half.astype(F32)
    own_u = temp * jnp.sum(img_wide * txt_wide, axis=1, keepdims=True) + shift
    own_sigmoid, own_softplus = sigmoid_and_softplus(-own_u)
    own_slope = -own_sigmoid * own_used
    own_pair = own_softplus * own_used
    own_weight = (own_slope * temp).astype(BF16).astype(F32)
    own_sums = (jnp.sum(own_pair), jnp.sum(own_slope), jnp.sum(own_slope * (own_u - shift)))

    halves = [(made,) for made in first]
    for k in range(1, 5):
        for n, r in enumerate(rings):
            for made in halves[n]:
                made.wait_recv()
            halves[n] = forward(r, 8, k, H0) if k < 4 else last_half(r)
        arrived = (RING - k, k) if k < 4 else (4,)
        for n, r in enumerate(rings):
            for made in whole[n]:
                made.wait_recv()
            if k < 3:
                whole[n] = forward(r, 0, k + 1, FULL)
            elif k == 3:
                whole[n] = last_whole(r)
            for s in arrived:
                second[n][s] = across(r, s, H1)
            if n == 0:
                core_got += [to_core(s) for s in arrived]
        for s in (RING - k + 1, k - 1) if k > 1 else (0,):
            second[0][s].wait_recv()
            core_got.append(to_core(8 + s))
    for n in range(2):
        for made in halves[n]:
            made.wait_recv()
    second[0][4].wait_recv()
    core_got.append(to_core(12))
    for made in second[1].values():
        made.wait_recv()
    for made in core_got:
        made.wait_recv()

    def block(c, sums):
        rows = pl.ds(pl.multiple_of(c * 256, 256), 256)
        logits[...] = lax.dot_general(
            txt[rows, :], img[...], (((1,), (1,)), ((), ())), preferred_element_type=F32
        )
        tx = jnp.where(lax.rem(c, 2) == 1, pair_t, x)
        tc = jnp.where(c >= 2, 1 - core, core)
        pair_sum, slope_sum, scaled_sum = sums
        for k in range(8):
            scaled = logits[tile(k), :] * temp
            u = scaled + shift
            slope, pair = sigmoid_and_softplus(u)
            if k == 0:
                row = lax.broadcasted_iota(jnp.int32, (T, 512), 0)
                column = lax.broadcasted_iota(jnp.int32, (T, 512), 1)
                own = (row == column) & (c == 0)
                slope = jnp.where(own, 0.0, slope)
                pair = jnp.where(own, 0.0, pair)
            weight[pl.ds(pl.multiple_of(c * 256 + k * T, T), T), :] = (slope * temp).astype(BF16)
            used = tile_used(tx, y, ring(z + k), tc)

            def folded(value):
                return jnp.sum(value.reshape(T // 8, 8, 512), axis=0)

            pair_sum = pair_sum + used * folded(pair)
            slope_sum = slope_sum + used * folded(slope)
            scaled_sum = scaled_sum + folded(slope * scaled)
        return pair_sum, slope_sum, scaled_sum

    zero = jnp.zeros((8, 512), F32)
    pair_sum, slope_sum, scaled_sum = lax.fori_loop(0, 4, block, (zero, zero, zero))

    column_tile = lax.broadcasted_iota(jnp.int32, (8, 512), 1) // T
    columns_used = zero
    for s in range(16):
        used = tile_used(x if s < 8 else pair_i, ring(y + s), z, core)
        columns_used = jnp.where(column_tile == s, used, columns_used)
    sums = (
        jnp.sum(pair_sum * columns_used) + own_sums[0],
        jnp.sum(slope_sum * columns_used) + own_sums[1],
        jnp.sum(scaled_sum) + own_sums[2],
    )
    lane = lax.broadcasted_iota(jnp.int32, (8, 128), 1)
    vector = jnp.where(lane == 0, sums[0], jnp.where(lane == 1, sums[1], jnp.where(lane == 2, sums[2], 0.0)))

    scal_sent = []

    def scalar_copy(stage, d, mine, slot, peer):
        return pltpu.make_async_remote_copy(
            src_ref=scal.at[stage, mine],
            dst_ref=scal.at[stage, slot],
            send_sem=ssem.at[SCAL + stage * 8 + d],
            recv_sem=rsem.at[SCAL + stage * 8 + slot],
            device_id=peer,
            device_id_type=MESH,
        )

    def spread(stage, mine, peer_of, value):
        scal[stage, mine] = value
        for d in range(1, RING):
            made = scalar_copy(stage, d, mine, mine, peer_of(d))
            made.start()
            scal_sent.append(made)

    def summed(stage, mine, peer_of):
        for d in range(1, RING):
            scalar_copy(stage, d, mine, ring(mine + d), peer_of(d)).wait_recv()
        total = scal[stage, 0]
        for k in range(1, RING):
            total = total + scal[stage, k]
        return total

    spread(0, y, y_peer, vector)

    def text_dir(first):
        return jnp.dot(weight[first : first + 256, :], img[...], preferred_element_type=F32)

    core_back = []
    for first in (256, 0):
        out_c[first : first + 256, :] = text_dir(512 + first).astype(BF16)
        part = pl.ds(first, 256)
        core_back.append(send(out_c.at[part], from_c.at[part], core_mate))
    for first in (256, 0):
        img_sum[first : first + 256, :] = lax.dot_general(
            weight[:, first : first + 256], txt[...], (((0,), (0,)), ((), ())), preferred_element_type=F32
        )
    for first in (256, 0):
        txt_sum[first : first + 256, :] = text_dir(first)

    total = summed(0, y, y_peer)
    spread(1, z, z_peer, total)

    for made in core_back:
        made.wait_recv()

    def img_own(slot, part):
        return img_sum[at(slot, part), :]

    def txt_own(slot, part):
        return txt_sum[at(slot, part), :] + from_c[at(slot, part), :].astype(F32)

    back = (
        (txt_own, txt_out, txt_back, z_peer(1), z_peer(RING - 1), txt_mate),
        (img_own, img_out, img_back, y_peer(1), y_peer(RING - 1), img_mate),
    )
    WHOLE, HALF, MATE, HOME = 0, 8 * T, 12 * T, 16 * T

    def landing(first, n):
        return pl.ds(first, n)

    def whole_place(way, k, part=FULL):
        return landing(WHOLE + (way * 4 + k - 1) * T + part[0], part[1])

    def half_place(way, k):
        return landing(HALF + (way * 4 + k - 1) * 16, 16)

    def mate_place(slot):
        return landing(MATE + slot * 16, 16)

    def emit(which, slot, part, value, place, peer):
        _, out, recv = which[:3]
        out[at(slot, part), :] = value.astype(BF16)
        return send(out.at[at(slot, part)], recv.at[place], peer)

    mate_got = [{}, {}]
    for s in (4, 3, 5, 2, 6, 1, 7, 0):
        for n, r in enumerate(back):
            mate_got[n][s] = emit(r, 8 + s, H1, r[0](8 + s, H1), mate_place(s), r[5])

    half_got, whole_got = [None, None], [None, None]
    for n, r in enumerate(back):
        way = toward((None, r[3], r[4], None))
        made = emit(r, 12, H0, r[0](12, H0), half_place(0, 1), way)
        half_got[n] = (made,)
    up = [emit(r, 4, H0, r[0](4, H0), whole_place(0, 1, H0), r[3]) for r in back]

    def from_mate(n, s):
        mate_got[n][s].wait_recv()
        return back[n][0](s, H1) + back[n][2][mate_place(s), :].astype(F32)

    for n, r in enumerate(back):
        down = emit(r, 4, H1, from_mate(n, 4), whole_place(1, 1, H1), r[4])
        whole_got[n] = (up[n], down)

    for k in range(2, 5):
        for n, r in enumerate(back):
            for made in half_got[n]:
                made.wait_recv()
            made = []
            for way, s in enumerate((5 - k, 3 + k)):
                value = r[0](8 + s, H0)
                if k == 2:
                    value = value + jnp.where(odd == way, r[2][half_place(0, 1), :].astype(F32), 0.0)
                else:
                    value = value + r[2][half_place(way, k - 1), :].astype(F32)
                made.append(emit(r, 8 + s, H0, value, half_place(way, k), r[3 + way]))
            half_got[n] = made
        for n, r in enumerate(back):
            made = []
            for way, s in enumerate((5 - k, 3 + k)):
                top, low = r[0](s, H0), from_mate(n, s)
                whole_got[n][way].wait_recv()
                if k > 2 or way == 0:
                    top = top + r[2][whole_place(way, k - 1, H0), :].astype(F32)
                if k > 2 or way == 1:
                    low = low + r[2][whole_place(way, k - 1, H1), :].astype(F32)
                r[1][at(s, H0), :] = top.astype(BF16)
                r[1][at(s, H1), :] = low.astype(BF16)
                made.append(send(r[1].at[at(s)], r[2].at[whole_place(way, k)], r[3 + way]))
            whole_got[n] = made
        if k == 2:
            total = summed(1, z, z_peer)
            spread(2, my_xc, xc_peer, total)

    home = []
    for n, r in enumerate(back):
        value = r[0](8, H0)
        for way in range(2):
            half_got[n][way].wait_recv()
            value = value + r[2][half_place(way, 4), :].astype(F32)
        home.append(emit(r, 8, H0, value, landing(HOME, 16), r[5]))

    total = summed(2, my_xc, xc_peer)
    used = lax.fori_loop(0, counts.shape[0], lambda i, sum: sum + counts[i], 0).astype(F32)
    means = total / used
    loss[0] = means[0, 0]
    grad_bias[0] = means[0, 1]
    grad_log_temp[0] = means[0, 2]

    ends = ((txt_unit, txt_length, img_wide, grad_txt), (img_unit, img_length, txt_wide, grad_img))
    for n, r in enumerate(back):
        unit, length, other, grad = ends[n]
        top, low = r[0](0, H0), from_mate(n, 0)
        for way in range(2):
            whole_got[n][way].wait_recv()
            top = top + r[2][whole_place(way, 4, H0), :].astype(F32)
            low = low + r[2][whole_place(way, 4, H1), :].astype(F32)
        home[n].wait_recv()
        top = top + r[2][landing(HOME, 16), :].astype(F32)
        total_dir = jnp.concatenate([top, low], axis=0) + own_weight * other
        total_dir = jnp.where(own_used > 0.0, total_dir, 0.0)
        grad[...] = projected(total_dir, unit, length)

    assert len(sent) <= SCAL
    for made in sent + scal_sent:
        made.wait_send()


def place_results(*refs):
    sources, targets, arrived = refs[:5], refs[5:10], refs[10]
    moved = [pltpu.make_async_copy(sources[k], targets[k], arrived.at[k]) for k in range(5)]
    for made in moved:
        made.start()
    for made in moved:
        made.wait()


def body(images, texts, row_counts, log_temp, bias):
    rows, width = images.shape
    scalar = jax.ShapeDtypeStruct((1,), F32)
    grad = jax.ShapeDtypeStruct((rows, width), F32)
    vmem = pl.BlockSpec(memory_space=pltpu.VMEM)
    smem = pl.BlockSpec(memory_space=pltpu.SMEM)
    found = pl.pallas_call(
        kernel,
        out_shape=(scalar, scalar, scalar, grad, grad),
        in_specs=[pl.BlockSpec(memory_space=pltpu.HBM)] * 5,
        out_specs=(smem, smem, smem, vmem, vmem),
        scratch_shapes=[
            pltpu.VMEM((T, width), BF16),
            pltpu.VMEM((T, width), BF16),
            pltpu.SMEM(row_counts.shape, jnp.int32),
            pltpu.SMEM((1,), F32),
            pltpu.SMEM((1,), F32),
            pltpu.VMEM((512, width), BF16),
            pltpu.VMEM((1024, width), BF16),
            pltpu.VMEM((1024, 512), BF16),
            pltpu.VMEM((256, 512), F32),
            pltpu.VMEM((512, width), BF16),
            pltpu.VMEM((512, width), BF16),
            pltpu.VMEM((512, width), F32),
            pltpu.VMEM((512, width), F32),
            pltpu.VMEM((512, width), BF16),
            pltpu.VMEM((512, width), BF16),
            pltpu.VMEM((17 * T, width), BF16),
            pltpu.VMEM((17 * T, width), BF16),
            pltpu.VMEM((3, 8, 8, 128), F32),
            pltpu.SemaphoreType.DMA((5,)),
            pltpu.SemaphoreType.DMA((N_SEM,)),
            pltpu.SemaphoreType.DMA((N_SEM,)),
        ],
        compiler_params=pltpu.CompilerParams(
            collective_id=0, has_side_effects=True, vmem_limit_bytes=60 << 20
        ),
        cost_estimate=pl.CostEstimate(flops=6 * 512 * 1024 * width, bytes_accessed=4 << 20, transcendentals=1 << 20),
    )(images, texts, row_counts, log_temp, bias)
    return pl.pallas_call(
        place_results,
        out_shape=(scalar, scalar, scalar, grad, grad),
        in_specs=[smem] * 3 + [vmem] * 2,
        out_specs=[pl.BlockSpec(memory_space=pltpu.HBM)] * 5,
        scratch_shapes=[pltpu.SemaphoreType.DMA((5,))],
    )(*found)


def solution(mesh):
    return jax.shard_map(
        body,
        mesh=mesh,
        in_specs=(P(("blk", "sub"), None), P(("blk", "sub"), None), P(), P(), P()),
        out_specs=(P(), P(), P(), P(("blk", "sub"), None), P(("blk", "sub"), None)),
        check_vma=False,
    )
```

time: 83.3 us -> 72.3 us (0.87)
  the two profiles are of different devices: /device:TPU:1 before, /device:TPU:8 now
where the time goes in v2:
time: 72.3 us; the launch traced here: 72.1 us
  Pallas kernels  70.1 us (97%)
  between operations  1.93 us (3%)
    pallas_call x1, Pallas kernels, body(): pl.pallas_call(kernel, out_shape=(scalar, scalar, scalar, grad, grad), in...  66.5 us
    pallas_call x1, Pallas kernels, body(): pl.pallas_call(place_results, out_shape=(scalar, scalar, scalar, grad, gr...  3.67 us

profile of v2, /device:TPU:8, one launch (start us, length us, event | category | flops | bytes accessed | tf_op | source)
XLA Modules:
  0.0 72.1 jit_solution(17964077146945104375)
XLA Ops:
  1.9 66.5 %shard_map.92 = (f32[1]{0:T(128)}, f32[1]{0:T(128)}, f32[1]{0:T(128)}, f32[32,1152]{1,0:T(8,128)}, f32[32,1152]{1,0:T(8,128)}) custom-call(bf16[32,1152]{1,0:T(8,128)(2,1)} %img_hbm.1, bf16[32,1152]{1,0:T(8,128)(2,1)} %txt_hbm.1, s32[128]{0:T(128)} %counts_hbm.1, f32[1]{0:T(128)S(6)} %copy.10.log_temp_hbm, f32[1]{0:T(128)S(6)} %copy.11.bias_hbm), custom_call_target="tpu_custom_call" | custom-call | flops 3623878656 | bytes 4194304 | tf_op jit(solution)/shard_map/pallas_call | solution.py:445
  68.4 3.7 %shard_map.93 = (f32[1]{0:T(128)}, f32[1]{0:T(128)}, f32[1]{0:T(128)}, f32[32,1152]{1,0:T(8,128)}, f32[32,1152]{1,0:T(8,128)}) custom-call(f32[1]{0:T(128)} %get-tuple-element.10.refs_0_, f32[1]{0:T(128)} %get-tuple-element.11.refs_1_, f32[1]{0:T(128)} %get-tuple-element.12.refs_2_, f32[32,1152]{1,0:T(8,128)} %get-tuple-element.13.refs_3_, ...), custom_call_target="tpu_custom_call" | custom-call | tf_op jit(solution)/shard_map/pallas_call | solution.py:478

commit v3 on v2

v3 whole, which is shorter than its diff:
```python
import functools

import jax
import jax.numpy as jnp
from jax import lax
from jax.experimental import pallas as pl
from jax.experimental.pallas import tpu as pltpu
from jax.sharding import PartitionSpec as P

MESH = pl.DeviceIdType.MESH
F32 = jnp.float32
BF16 = jnp.bfloat16
T = 32
RING = 8
N_SEM = 192
SCAL = 160
FULL = (0, T)
PIECES = ((0, 16), (16, 16))
OWN, MATE = 0, 1
ROUTES = (
    ({1: 0, 2: 0, 3: 2, 4: 3}, {0: None, 1: None, 2: None, 3: None, 4: 2}),
    ({1: 0, 2: 1, 3: 2, 4: 2}, {0: None, 1: 0, 2: None, 3: 1, 4: 3}),
)
CORE = 2
GATHER = (
    (MATE, 1, 0), (OWN, 1, 1), (OWN, 0, 2), (OWN, 0, 1), (MATE, 0, 0), (CORE, OWN, 0), (MATE, 1, 1), (CORE, MATE, 0),
    (OWN, 1, 2), (MATE, 0, 1), (OWN, 0, 3), (MATE, 0, 2), (CORE, OWN, 1), (MATE, 1, 3), (OWN, 1, 3), (OWN, 1, 4),
    (MATE, 1, 2), (CORE, OWN, 2), (MATE, 0, 3), (OWN, 0, 4), (CORE, MATE, 1), (MATE, 0, 4), (MATE, 1, 4),
    (CORE, OWN, 3), (CORE, MATE, 2), (CORE, OWN, 4), (CORE, MATE, 3), (CORE, MATE, 4),
)
REDUCE = (
    (MATE, 0, 4), (MATE, 1, 4), (MATE, 0, 3), (OWN, 0, 4), (MATE, 1, 2), (OWN, 1, 3), (OWN, 1, 4), (MATE, 1, 3),
    (MATE, 0, 2), (MATE, 0, 1), (OWN, 0, 3), (OWN, 1, 2), (MATE, 1, 1), (OWN, 0, 2), (OWN, 0, 1), (OWN, 1, 1),
    (MATE, 1, 0), (MATE, 0, 0),
)
ORDER = (12, 11, 13, 4, 10, 14, 5, 3, 9, 15, 6, 2, 7, 1, 8, 0)


def ways(k):
    return (0, 1) if 0 < k < 4 else (0,)


def ring_slot(k, way):
    return (RING - k) % RING if way == 0 else k


def place():
    blk, sub = lax.axis_index("blk"), lax.axis_index("sub")
    core = lax.rem(blk, 2)
    y = lax.rem(lax.div(blk, 2), RING)
    z = lax.rem(lax.div(blk, 16), 2) * 4 + sub
    x = lax.div(blk, 32)
    return x, y, z, core


def member(x, y, z, core):
    return ((x * 2 + lax.div(z, 4)) * RING + y) * 2 + core


def device(x, y, z, core):
    return (member(x, y, z, core), lax.rem(z, 4))


def ring(value):
    return lax.rem(value, RING)


def normalized(values):
    wide = values.astype(F32)
    length = jnp.sqrt(jnp.sum(wide * wide, axis=1, keepdims=True) + 1e-06)
    return wide / length, length


def projected(grad, unit, length):
    return (grad - unit * jnp.sum(unit * grad, axis=1, keepdims=True)) / length


def sigmoid_and_softplus(u):
    small = jnp.exp(-jnp.abs(u))
    ratio = 1.0 / (1.0 + small)
    sigmoid = jnp.where(u >= 0.0, ratio, small * ratio)
    softplus = jnp.maximum(u, 0.0) + jnp.log1p(small)
    return sigmoid, softplus


def at(slot, part=FULL):
    return pl.ds((slot // 16 * 16 + ORDER.index(slot % 16)) * T + part[0], part[1])


def tile(slot):
    return pl.ds(slot * T, T)


def kernel(
    img_hbm, txt_hbm, counts_hbm, log_temp_hbm, bias_hbm,
    loss, grad_log_temp, grad_bias, grad_img, grad_txt,
    img_in, txt_in, counts, log_temp, bias, img, txt, weight, logits,
    out_c, from_c, img_sum, txt_sum, img_out, txt_out, img_back, txt_back, scal, local, ssem, rsem,
):
    x, y, z, core = place()
    pair_i = x + 1 - 2 * lax.rem(x, 2)
    pair_t = lax.rem(x + 3 + 2 * lax.rem(x, 2), 4)

    def y_peer(d):
        return device(x, ring(y + RING + d), z, core)

    def z_peer(d):
        return device(x, y, ring(z + RING + d), core)

    my_xc = x * 2 + core

    def xc_peer(d):
        other = ring(my_xc + d)
        return device(lax.div(other, 2), y, z, lax.rem(other, 2))

    img_mate = device(pair_i, y, z, core)
    txt_mate = device(pair_t, y, z, core)
    core_mate = device(x, y, z, 1 - core)

    fetched = [
        pltpu.make_async_copy(source, target, local.at[k])
        for k, (source, target) in enumerate(
            ((counts_hbm, counts), (log_temp_hbm, log_temp), (bias_hbm, bias), (img_hbm, img_in), (txt_hbm, txt_in))
        )
    ]
    for made in fetched:
        made.start()

    barrier = pltpu.get_barrier_semaphore()
    for d in range(1, RING):
        for peer in (y_peer(d), z_peer(d), xc_peer(d)):
            pl.semaphore_signal(barrier, inc=1, device_id=peer, device_id_type=MESH)

    for made in fetched:
        made.wait()

    temp = jnp.exp(jnp.full((1, 1), log_temp[0], F32))
    shift = bias[0]
    img_unit, img_length = normalized(img_in[...])
    txt_unit, txt_length = normalized(txt_in[...])

    def tile_used(x, y, z, core):
        return jnp.where(counts[member(x, y, z, core)] > T * lax.rem(z, 4), 1.0, 0.0)

    own_used = tile_used(x, y, z, core)
    img_half = jnp.where(own_used > 0.0, img_unit, 0.0).astype(BF16)
    txt_half = jnp.where(own_used > 0.0, txt_unit, 0.0).astype(BF16)
    img[at(0), :] = img_half
    txt[at(0), :] = txt_half

    sent = []

    def send(src, dst, peer):
        index = len(sent)
        made = pltpu.make_async_remote_copy(
            src_ref=src,
            dst_ref=dst,
            send_sem=ssem.at[index],
            recv_sem=rsem.at[index],
            device_id=peer,
            device_id_type=MESH,
        )
        made.start()
        sent.append(made)
        return made

    odd = lax.rem(core, 2)
    TXT, IMG = 0, 1
    ring_buf, ring_peer, ring_mate = (txt, img), (z_peer, y_peer), (txt_mate, img_mate)

    pl.semaphore_wait(barrier, 3 * (RING - 1))

    gathered = {}

    def way_on(ring, k, parent):
        return ring_peer[ring](jnp.where(odd == 1, parent - k, k - parent))

    def move(ring, column, piece, k):
        buf, part = ring_buf[ring], PIECES[piece]
        parent, made = ROUTES[piece][column][k], []
        for way in ways(k):
            slot = ring_slot(k, way)
            if parent is None:
                source, target, peer = at(slot, part), at(8 + slot, part), ring_mate[ring]
            elif k < 4:
                source, target = at(column * 8 + ring_slot(parent, way), part), at(column * 8 + slot, part)
                peer = ring_peer[ring]((k - parent) * (1 - 2 * way))
            else:
                up, down = (ORDER.index(column * 8 + ring_slot(parent, w)) for w in (0, 1))
                first = jnp.where(odd == 1, down, up) * T + part[0]
                source, target = pl.ds(pl.multiple_of(first, 16), 16), at(column * 8 + slot, part)
                peer = way_on(ring, k, parent)
            made.append(send(buf.at[source], buf.at[target], peer))
        gathered[ring, column, piece, k] = made

    def arrive(*key):
        for made in gathered.get(key, ()):
            made.wait_recv()
        gathered[key] = ()

    def run(column, piece, k):
        if column == CORE:
            base = piece * 8
            if k or base:
                for n in range(2):
                    arrive(TXT, piece, n, k)
            gathered[TXT, CORE, piece, k] = [
                send(txt.at[at(base + ring_slot(k, way))], txt.at[at(16 + base + ring_slot(k, way))], core_mate)
                for way in ways(k)
            ]
            return
        parent = ROUTES[piece][column][k]
        for n in (TXT, IMG):
            if parent is None and k:
                arrive(n, OWN, piece, k)
            elif parent is not None and (parent or column == MATE):
                arrive(n, column, piece, parent)
            move(n, column, piece, k)

    at_once = 6
    for entry in GATHER[:at_once]:
        run(*entry)

    img_wide, txt_wide = img_half.astype(F32), txt_half.astype(F32)
    own_u = temp * jnp.sum(img_wide * txt_wide, axis=1, keepdims=True) + shift
    own_sigmoid, own_softplus = sigmoid_and_softplus(-own_u)
    own_slope = -own_sigmoid * own_used
    own_pair = own_softplus * own_used
    own_weight = (own_slope * temp).astype(BF16).astype(F32)
    own_sums = [jnp.sum(value, axis=0, keepdims=True) for value in (own_pair, own_slope, own_slope * (own_u - shift))]
    used = lax.fori_loop(0, counts.shape[0], lambda i, sum: sum + counts[i], 0).astype(F32)

    column_tile = lax.broadcasted_iota(jnp.int32, (8, 512), 1) // T
    columns_used = jnp.zeros((8, 512), F32)
    for k, s in enumerate(ORDER):
        columns_used = jnp.where(
            column_tile == k, tile_used(x if s < 8 else pair_i, ring(y + s), z, core), columns_used
        )

    for entry in GATHER[at_once:]:
        run(*entry)
    for key in tuple(gathered):
        arrive(*key)

    def block(c, sums):
        rows = pl.ds(pl.multiple_of(c * 256, 256), 256)
        logits[...] = lax.dot_general(
            txt[rows, :], img[...], (((1,), (1,)), ((), ())), preferred_element_type=F32
        )
        late = lax.rem(c, 2) == 1
        tc = jnp.where(c >= 2, 1 - core, core)
        pair_sum, slope_sum, scaled_sum = sums
        for k in range(8):
            scaled = logits[tile(k), :] * temp
            u = scaled + shift
            slope, pair = sigmoid_and_softplus(u)
            if k == 7:
                row = lax.broadcasted_iota(jnp.int32, (T, 512), 0)
                column = lax.broadcasted_iota(jnp.int32, (T, 512), 1)
                own = (row + 15 * T == column) & (c == 1)
                slope = jnp.where(own, 0.0, slope)
                pair = jnp.where(own, 0.0, pair)
            weight[pl.ds(pl.multiple_of(c * 256 + k * T, T), T), :] = (slope * temp).astype(BF16)
            slot = jnp.where(late, ORDER[8 + k], ORDER[k])
            used = tile_used(jnp.where(slot >= 8, pair_t, x), y, ring(z + slot), tc)

            def folded(value):
                return jnp.sum(value.reshape(T // 8, 8, 512), axis=0)

            pair_sum = pair_sum + used * folded(pair)
            slope_sum = slope_sum + used * folded(slope)
            scaled_sum = scaled_sum + folded(slope * scaled)
        return pair_sum, slope_sum, scaled_sum

    zero = jnp.zeros((8, 512), F32)
    pair_sum, slope_sum, scaled_sum = lax.fori_loop(0, 4, block, (zero, zero, zero))

    lane = lax.broadcasted_iota(jnp.int32, (8, 128), 1)

    def own_total():
        whole = [
            jnp.sum(value, axis=(0, 1), keepdims=True)
            for value in (pair_sum * columns_used, slope_sum * columns_used, scaled_sum)
        ]
        vector = jnp.zeros((8, 128), F32)
        for k in range(3):
            vector = jnp.where(lane == k, whole[k] + own_sums[k], vector)
        return vector

    scal_sent = []

    def scalar_copy(stage, d, mine, slot, peer):
        return pltpu.make_async_remote_copy(
            src_ref=scal.at[stage, mine],
            dst_ref=scal.at[stage, slot],
            send_sem=ssem.at[SCAL + stage * 8 + d],
            recv_sem=rsem.at[SCAL + stage * 8 + slot],
            device_id=peer,
            device_id_type=MESH,
        )

    def spread(stage, mine, peer_of, value):
        scal[stage, mine] = value
        for d in range(1, RING):
            made = scalar_copy(stage, d, mine, mine, peer_of(d))
            made.start()
            scal_sent.append(made)

    def summed(stage, mine, peer_of):
        for d in range(1, RING):
            scalar_copy(stage, d, mine, ring(mine + d), peer_of(d)).wait_recv()
        total = scal[stage, 0]
        for k in range(1, RING):
            total = total + scal[stage, k]
        return total

    def rows_of(group):
        return pl.ds(group * 128, 128)

    def text_dir(first):
        return jnp.dot(weight[first : first + 128, :], img[...], preferred_element_type=F32)

    core_back = {}

    def other_texts(group):
        out_c[rows_of(group), :] = text_dir(512 + group * 128).astype(BF16)
        core_back[group] = send(out_c.at[rows_of(group)], from_c.at[rows_of(group)], core_mate)

    def own_images(group):
        img_sum[rows_of(group), :] = lax.dot_general(
            weight[:, group * 128 : group * 128 + 128], txt[...], (((0,), (0,)), ((), ())), preferred_element_type=F32
        )

    def own_texts(group):
        txt_sum[rows_of(group), :] = text_dir(group * 128)

    computed = set()

    def compute(group):
        if group not in computed:
            computed.add(group)
            if group == 0:
                other_texts(0)
            own_images(group)
            if group < 3:
                other_texts(group + 1)
            own_texts(group)

    core_seen = set()

    def own_part(ring, slot, part):
        group = ORDER.index(slot) // 4
        compute(group)
        if ring == IMG:
            return img_sum[at(slot, part), :]
        if group not in core_seen:
            core_seen.add(group)
            core_back[group].wait_recv()
        return txt_sum[at(slot, part), :] + from_c[at(slot, part), :].astype(F32)

    out, back = (txt_out, img_out), (txt_back, img_back)
    coming, places = {}, {}

    def landing(column, piece, k, way):
        row = places.setdefault((column, piece, k, way), len(places) * 16)
        return pl.ds(row, 16)

    def received(ring, column, piece, k, way):
        key = (ring, column, piece, k, way)
        if coming[key] is not None:
            coming[key].wait_recv()
            coming[key] = None
        return back[ring][landing(column, piece, k, way), :].astype(F32)

    def partial(ring, column, piece, k, way):
        value = own_part(ring, column * 8 + ring_slot(k, way), PIECES[piece])
        if column == OWN and ROUTES[piece][MATE][k] is None:
            value = value + received(ring, MATE, piece, k, way)
        for further, parent in ROUTES[piece][column].items():
            if parent != k:
                continue
            if further < 4:
                for w in (0, 1) if k == 0 else (way,):
                    value = value + received(ring, column, piece, further, w)
            else:
                extra = received(ring, column, piece, 4, 0)
                value = value + (extra if k == 0 else jnp.where(odd == way, extra, 0.0))
        return value

    def pass_back(ring, column, piece, k):
        parent, part = ROUTES[piece][column][k], PIECES[piece]
        for way in ways(k):
            slot = column * 8 + ring_slot(k, way)
            out[ring][at(slot, part), :] = partial(ring, column, piece, k, way).astype(BF16)
            if parent is None:
                peer = ring_mate[ring]
            elif k < 4:
                peer = ring_peer[ring]((parent - k) * (1 - 2 * way))
            else:
                peer = ring_peer[ring](jnp.where(odd == 1, k - parent, parent - k))
            target = back[ring].at[landing(column, piece, k, way)]
            coming[ring, column, piece, k, way] = send(out[ring].at[at(slot, part)], target, peer)

    for n, entry in enumerate(REDUCE):
        for which in (IMG, TXT):
            pass_back(which, *entry)
        if n == 1:
            spread(0, y, y_peer, own_total())
        elif n == 8:
            spread(1, z, z_peer, summed(0, y, y_peer))
        elif n == 13:
            spread(2, my_xc, xc_peer, summed(1, z, z_peer))

    total = summed(2, my_xc, xc_peer)
    means = total / used
    loss[0] = means[0, 0]
    grad_bias[0] = means[0, 1]
    grad_log_temp[0] = means[0, 2]

    ends = ((txt_unit, txt_length, img_wide, grad_txt), (img_unit, img_length, txt_wide, grad_img))
    for n in (TXT, IMG):
        unit, length, other, grad = ends[n]
        top, low = (partial(n, OWN, piece, 0, 0) for piece in (0, 1))
        total_dir = jnp.concatenate([top, low], axis=0) + own_weight * other
        total_dir = jnp.where(own_used > 0.0, total_dir, 0.0)
        grad[...] = projected(total_dir, unit, length)

    assert len(sent) <= SCAL and len(places) * 16 <= back[0].shape[0]
    for made in sent + scal_sent:
        made.wait_send()


def place_results(*refs):
    sources, targets, arrived = refs[:5], refs[5:10], refs[10]
    moved = [pltpu.make_async_copy(sources[k], targets[k], arrived.at[k]) for k in range(5)]
    for made in moved:
        made.start()
    for made in moved:
        made.wait()


def body(images, texts, row_counts, log_temp, bias):
    rows, width = images.shape
    scalar = jax.ShapeDtypeStruct((1,), F32)
    grad = jax.ShapeDtypeStruct((rows, width), F32)
    vmem = pl.BlockSpec(memory_space=pltpu.VMEM)
    smem = pl.BlockSpec(memory_space=pltpu.SMEM)
    found = pl.pallas_call(
        kernel,
        out_shape=(scalar, scalar, scalar, grad, grad),
        in_specs=[pl.BlockSpec(memory_space=pltpu.HBM)] * 5,
        out_specs=(smem, smem, smem, vmem, vmem),
        scratch_shapes=[
            pltpu.VMEM((T, width), BF16),
            pltpu.VMEM((T, width), BF16),
            pltpu.SMEM(row_counts.shape, jnp.int32),
            pltpu.SMEM((1,), F32),
            pltpu.SMEM((1,), F32),
            pltpu.VMEM((512, width), BF16),
            pltpu.VMEM((1024, width), BF16),
            pltpu.VMEM((1024, 512), BF16),
            pltpu.VMEM((256, 512), F32),
            pltpu.VMEM((512, width), BF16),
            pltpu.VMEM((512, width), BF16),
            pltpu.VMEM((512, width), F32),
            pltpu.VMEM((512, width), F32),
            pltpu.VMEM((512, width), BF16),
            pltpu.VMEM((512, width), BF16),
            pltpu.VMEM((480, width), BF16),
            pltpu.VMEM((480, width), BF16),
            pltpu.VMEM((3, 8, 8, 128), F32),
            pltpu.SemaphoreType.DMA((5,)),
            pltpu.SemaphoreType.DMA((N_SEM,)),
            pltpu.SemaphoreType.DMA((N_SEM,)),
        ],
        compiler_params=pltpu.CompilerParams(
            collective_id=0, has_side_effects=True, vmem_limit_bytes=60 << 20
        ),
        cost_estimate=pl.CostEstimate(flops=6 * 512 * 1024 * width, bytes_accessed=4 << 20, transcendentals=1 << 20),
    )(images, texts, row_counts, log_temp, bias)
    return pl.pallas_call(
        place_results,
        out_shape=(scalar, scalar, scalar, grad, grad),
        in_specs=[smem] * 3 + [vmem] * 2,
        out_specs=[pl.BlockSpec(memory_space=pltpu.HBM)] * 5,
        scratch_shapes=[pltpu.SemaphoreType.DMA((5,))],
    )(*found)


def solution(mesh):
    return jax.shard_map(
        body,
        mesh=mesh,
        in_specs=(P(("blk", "sub"), None), P(("blk", "sub"), None), P(), P(), P()),
        out_specs=(P(), P(), P(), P(("blk", "sub"), None), P(("blk", "sub"), None)),
        check_vma=False,
    )
```

time: 72.3 us -> 64 us (0.89)
  the two profiles are of different devices: /device:TPU:8 before, /device:TPU:1 now
where the time goes in v3:
time: 64 us; the launch traced here: 63.1 us
  Pallas kernels  61.1 us (95%)
  between operations  1.93 us (3%)
    pallas_call x1, Pallas kernels, body(): pl.pallas_call(kernel, out_shape=(scalar, scalar, scalar, grad, grad), in...  57.5 us
    pallas_call x1, Pallas kernels, body(): pl.pallas_call(place_results, out_shape=(scalar, scalar, scalar, grad, gr...  3.67 us

profile of v3, /device:TPU:1, one launch (start us, length us, event | category | flops | bytes accessed | tf_op | source)
XLA Modules:
  0.0 63.1 jit_solution(7060818951082704005)
XLA Ops:
  1.9 57.5 %shard_map.92 = (f32[1]{0:T(128)}, f32[1]{0:T(128)}, f32[1]{0:T(128)}, f32[32,1152]{1,0:T(8,128)}, f32[32,1152]{1,0:T(8,128)}) custom-call(bf16[32,1152]{1,0:T(8,128)(2,1)} %img_hbm.1, bf16[32,1152]{1,0:T(8,128)(2,1)} %txt_hbm.1, s32[128]{0:T(128)} %counts_hbm.1, f32[1]{0:T(128)S(6)} %copy.10.log_temp_hbm, f32[1]{0:T(128)S(6)} %copy.11.bias_hbm), custom_call_target="tpu_custom_call" | custom-call | flops 3623878656 | bytes 4194304 | tf_op jit(solution)/shard_map/pallas_call | solution.py:448
  59.4 3.7 %shard_map.93 = (f32[1]{0:T(128)}, f32[1]{0:T(128)}, f32[1]{0:T(128)}, f32[32,1152]{1,0:T(8,128)}, f32[32,1152]{1,0:T(8,128)}) custom-call(f32[1]{0:T(128)} %get-tuple-element.10.refs_0_, f32[1]{0:T(128)} %get-tuple-element.11.refs_1_, f32[1]{0:T(128)} %get-tuple-element.12.refs_2_, f32[32,1152]{1,0:T(8,128)} %get-tuple-element.13.refs_3_, ...), custom_call_target="tpu_custom_call" | custom-call | tf_op jit(solution)/shard_map/pallas_call | solution.py:481

commit v4 on v3

--- a/solution.py
+++ b/solution.py
@@ -93,7 +93,7 @@
 
 def kernel(
     img_hbm, txt_hbm, counts_hbm, log_temp_hbm, bias_hbm,
-    loss, grad_log_temp, grad_bias, grad_img, grad_txt,
+    scalars, grad_img, grad_txt,
     img_in, txt_in, counts, log_temp, bias, img, txt, weight, logits,
     out_c, from_c, img_sum, txt_sum, img_out, txt_out, img_back, txt_back, scal, local, ssem, rsem,
 ):
@@ -120,7 +120,7 @@
     fetched = [
         pltpu.make_async_copy(source, target, local.at[k])
         for k, (source, target) in enumerate(
-            ((counts_hbm, counts), (log_temp_hbm, log_temp), (bias_hbm, bias), (img_hbm, img_in), (txt_hbm, txt_in))
+            ((txt_hbm, txt_in), (img_hbm, img_in), (counts_hbm, counts), (log_temp_hbm, log_temp), (bias_hbm, bias))
         )
     ]
     for made in fetched:
@@ -131,21 +131,12 @@
         for peer in (y_peer(d), z_peer(d), xc_peer(d)):
             pl.semaphore_signal(barrier, inc=1, device_id=peer, device_id_type=MESH)
 
-    for made in fetched:
-        made.wait()
-
-    temp = jnp.exp(jnp.full((1, 1), log_temp[0], F32))
-    shift = bias[0]
-    img_unit, img_length = normalized(img_in[...])
-    txt_unit, txt_length = normalized(txt_in[...])
-
     def tile_used(x, y, z, core):
         return jnp.where(counts[member(x, y, z, core)] > T * lax.rem(z, 4), 1.0, 0.0)
 
-    own_used = tile_used(x, y, z, core)
-    img_half = jnp.where(own_used > 0.0, img_unit, 0.0).astype(BF16)
-    txt_half = jnp.where(own_used > 0.0, txt_unit, 0.0).astype(BF16)
-    img[at(0), :] = img_half
+    fetched[0].wait()
+    txt_unit, txt_length = normalized(txt_in[...])
+    txt_half = txt_unit.astype(BF16)
     txt[at(0), :] = txt_half
 
     sent = []
@@ -198,8 +189,10 @@
             made.wait_recv()
         gathered[key] = ()
 
-    def run(column, piece, k):
+    def run(column, piece, k, rings=(0, 1)):
         if column == CORE:
+            if TXT not in rings:
+                return
             base = piece * 8
             if k or base:
                 for n in range(2):
@@ -210,7 +203,7 @@
             ]
             return
         parent = ROUTES[piece][column][k]
-        for n in (TXT, IMG):
+        for n in rings:
             if parent is None and k:
                 arrive(n, OWN, piece, k)
             elif parent is not None and (parent or column == MATE):
@@ -219,7 +212,18 @@
 
     at_once = 6
     for entry in GATHER[:at_once]:
-        run(*entry)
+        run(*entry, rings=(TXT,))
+    fetched[1].wait()
+    img_unit, img_length = normalized(img_in[...])
+    img_half = img_unit.astype(BF16)
+    img[at(0), :] = img_half
+    for entry in GATHER[:at_once]:
+        run(*entry, rings=(IMG,))
+    for made in fetched[2:]:
+        made.wait()
+    own_used = tile_used(x, y, z, core)
+    temp = jnp.exp(jnp.full((1, 1), log_temp[0], F32))
+    shift = bias[0]
 
     img_wide, txt_wide = img_half.astype(F32), txt_half.astype(F32)
     own_u = temp * jnp.sum(img_wide * txt_wide, axis=1, keepdims=True) + shift
@@ -240,47 +244,60 @@
     for entry in GATHER[at_once:]:
         run(*entry)
     for key in tuple(gathered):
-        arrive(*key)
+        if key[0] == IMG:
+            arrive(*key)
+
+    def arrive_texts(c):
+        for key in tuple(gathered):
+            _, column, piece, k = key
+            base = (piece if column == CORE else column) * 8
+            early = ORDER.index(base + ring_slot(k, 0)) >= 8
+            if key[0] == TXT and early == (c % 2 == 1) and (column == CORE) == (c >= 2):
+                arrive(*key)
 
     def block(c, sums):
-        rows = pl.ds(pl.multiple_of(c * 256, 256), 256)
-        logits[...] = lax.dot_general(
-            txt[rows, :], img[...], (((1,), (1,)), ((), ())), preferred_element_type=F32
-        )
-        late = lax.rem(c, 2) == 1
-        tc = jnp.where(c >= 2, 1 - core, core)
+        turn = logits.at[c % 2]
+        turn[...] = lax.dot_general(
+            txt[pl.ds(c * 256, 256), :], img[...], (((1,), (1,)), ((), ())), preferred_element_type=F32
+        )
+        tc = core if c < 2 else 1 - core
         pair_sum, slope_sum, scaled_sum = sums
         for k in range(8):
-            scaled = logits[tile(k), :] * temp
+            scaled = turn[tile(k), :] * temp
             u = scaled + shift
             slope, pair = sigmoid_and_softplus(u)
-            if k == 7:
+            if (c, k) == (1, 7):
                 row = lax.broadcasted_iota(jnp.int32, (T, 512), 0)
                 column = lax.broadcasted_iota(jnp.int32, (T, 512), 1)
-                own = (row + 15 * T == column) & (c == 1)
+                own = row + 15 * T == column
                 slope = jnp.where(own, 0.0, slope)
                 pair = jnp.where(own, 0.0, pair)
-            weight[pl.ds(pl.multiple_of(c * 256 + k * T, T), T), :] = (slope * temp).astype(BF16)
-            slot = jnp.where(late, ORDER[8 + k], ORDER[k])
-            used = tile_used(jnp.where(slot >= 8, pair_t, x), y, ring(z + slot), tc)
+            slot = ORDER[c % 2 * 8 + k]
+            used = tile_used(pair_t if slot >= 8 else x, y, ring(z + slot), tc)
+            weight[pl.ds(c * 256 + k * T, T), :] = (slope * (columns_used[:1] * used * temp)).astype(BF16)
 
             def folded(value):
                 return jnp.sum(value.reshape(T // 8, 8, 512), axis=0)
 
             pair_sum = pair_sum + used * folded(pair)
             slope_sum = slope_sum + used * folded(slope)
-            scaled_sum = scaled_sum + folded(slope * scaled)
+            scaled_sum = scaled_sum + used * folded(slope * scaled)
         return pair_sum, slope_sum, scaled_sum
 
     zero = jnp.zeros((8, 512), F32)
-    pair_sum, slope_sum, scaled_sum = lax.fori_loop(0, 4, block, (zero, zero, zero))
+    totals = (zero, zero, zero)
+    for c in range(4):
+        arrive_texts(c)
+    for c in (1, 0, 3, 2):
+        totals = block(c, totals)
+    pair_sum, slope_sum, scaled_sum = totals
 
     lane = lax.broadcasted_iota(jnp.int32, (8, 128), 1)
 
     def own_total():
         whole = [
-            jnp.sum(value, axis=(0, 1), keepdims=True)
-            for value in (pair_sum * columns_used, slope_sum * columns_used, scaled_sum)
+            jnp.sum(value * columns_used, axis=(0, 1), keepdims=True)
+            for value in (pair_sum, slope_sum, scaled_sum)
         ]
         vector = jnp.zeros((8, 128), F32)
         for k in range(3):
@@ -336,21 +353,22 @@
 
     computed = set()
 
-    def compute(group):
-        if group not in computed:
-            computed.add(group)
-            if group == 0:
-                other_texts(0)
+    def compute(ring, group):
+        if (ring, group) in computed:
+            return
+        computed.add((ring, group))
+        if ring == IMG:
             own_images(group)
+        else:
+            own_texts(group)
             if group < 3:
                 other_texts(group + 1)
-            own_texts(group)
 
     core_seen = set()
 
     def own_part(ring, slot, part):
         group = ORDER.index(slot) // 4
-        compute(group)
+        compute(ring, group)
         if ring == IMG:
             return img_sum[at(slot, part), :]
         if group not in core_seen:
@@ -401,28 +419,29 @@
             target = back[ring].at[landing(column, piece, k, way)]
             coming[ring, column, piece, k, way] = send(out[ring].at[at(slot, part)], target, peer)
 
-    for n, entry in enumerate(REDUCE):
-        for which in (IMG, TXT):
-            pass_back(which, *entry)
-        if n == 1:
+    ahead = 0
+    other_texts(0)
+    for n in range(len(REDUCE) + ahead):
+        if n < len(REDUCE):
+            pass_back(IMG, *REDUCE[n])
+        if n >= ahead:
+            pass_back(TXT, *REDUCE[n - ahead])
+        if n == 3:
             spread(0, y, y_peer, own_total())
-        elif n == 8:
+        elif n == 10:
             spread(1, z, z_peer, summed(0, y, y_peer))
-        elif n == 13:
+        elif n == 15:
             spread(2, my_xc, xc_peer, summed(1, z, z_peer))
 
     total = summed(2, my_xc, xc_peer)
     means = total / used
-    loss[0] = means[0, 0]
-    grad_bias[0] = means[0, 1]
-    grad_log_temp[0] = means[0, 2]
+    scalars[...] = means
 
     ends = ((txt_unit, txt_length, img_wide, grad_txt), (img_unit, img_length, txt_wide, grad_img))
     for n in (TXT, IMG):
         unit, length, other, grad = ends[n]
         top, low = (partial(n, OWN, piece, 0, 0) for piece in (0, 1))
         total_dir = jnp.concatenate([top, low], axis=0) + own_weight * other
-        total_dir = jnp.where(own_used > 0.0, total_dir, 0.0)
         grad[...] = projected(total_dir, unit, length)
 
     assert len(sent) <= SCAL and len(places) * 16 <= back[0].shape[0]
@@ -430,11 +449,24 @@
         made.wait_send()
 
 
-def place_results(*refs):
-    sources, targets, arrived = refs[:5], refs[5:10], refs[10]
-    moved = [pltpu.make_async_copy(sources[k], targets[k], arrived.at[k]) for k in range(5)]
-    for made in moved:
+def place_results(scalars, grad_img, grad_txt, loss, grad_log_temp, grad_bias, img_out, txt_out, staged, arrived):
+    moved = [
+        pltpu.make_async_copy(source, target, arrived.at[k])
+        for k, (source, target) in enumerate(
+            (
+                (grad_img, img_out),
+                (grad_txt, txt_out),
+                (staged.at[0], loss),
+                (staged.at[1], grad_bias),
+                (staged.at[2], grad_log_temp),
+            )
+        )
+    ]
+    for made in moved[:2]:
         made.start()
+    for k in range(3):
+        staged[k, 0] = scalars[0, k]
+        moved[2 + k].start()
     for made in moved:
         made.wait()
 
@@ -444,12 +476,11 @@
     scalar = jax.ShapeDtypeStruct((1,), F32)
     grad = jax.ShapeDtypeStruct((rows, width), F32)
     vmem = pl.BlockSpec(memory_space=pltpu.VMEM)
-    smem = pl.BlockSpec(memory_space=pltpu.SMEM)
     found = pl.pallas_call(
         kernel,
-        out_shape=(scalar, scalar, scalar, grad, grad),
+        out_shape=(jax.ShapeDtypeStruct((8, 128), F32), grad, grad),
         in_specs=[pl.BlockSpec(memory_space=pltpu.HBM)] * 5,
-        out_specs=(smem, smem, smem, vmem, vmem),
+        out_specs=(vmem, vmem, vmem),
         scratch_shapes=[
             pltpu.VMEM((T, width), BF16),
             pltpu.VMEM((T, width), BF16),
@@ -459,7 +490,7 @@
             pltpu.VMEM((512, width), BF16),
             pltpu.VMEM((1024, width), BF16),
             pltpu.VMEM((1024, 512), BF16),
-            pltpu.VMEM((256, 512), F32),
+            pltpu.VMEM((2, 256, 512), F32),
             pltpu.VMEM((512, width), BF16),
             pltpu.VMEM((512, width), BF16),
             pltpu.VMEM((512, width), F32),
@@ -481,9 +512,9 @@
     return pl.pallas_call(
         place_results,
         out_shape=(scalar, scalar, scalar, grad, grad),
-        in_specs=[smem] * 3 + [vmem] * 2,
+        in_specs=[vmem] * 3,
         out_specs=[pl.BlockSpec(memory_space=pltpu.HBM)] * 5,
-        scratch_shapes=[pltpu.SemaphoreType.DMA((5,))],
+        scratch_shapes=[pltpu.SMEM((3, 1), F32), pltpu.SemaphoreType.DMA((5,))],
     )(*found)
 
 

time: 64 us -> 60.6 us (0.947)
  Pallas kernels: 61.1 us -> 58.3 us
    pallas_call x1, Pallas kernels: 3.67 us -> 1.77 us  [body(): pl.pallas_call(place_results, out_shape=(scalar, scalar, scalar, grad, gr...]
    pallas_call x1, Pallas kernels: 57.5 us -> 56.5 us  [body(): pl.pallas_call(kernel, out_shape=(jax.ShapeDtypeStruct((8, 128), F32), gr...]
where the time goes in v4:
time: 60.6 us; the launch traced here: 60.2 us
  Pallas kernels  58.3 us (96%)
  between operations  1.93 us (3%)
    pallas_call x1, Pallas kernels, body(): pl.pallas_call(kernel, out_shape=(jax.ShapeDtypeStruct((8, 128), F32), gr...  56.5 us
    pallas_call x1, Pallas kernels, body(): pl.pallas_call(place_results, out_shape=(scalar, scalar, scalar, grad, gr...  1.77 us

profile of v4, /device:TPU:1, one launch (start us, length us, event | category | flops | bytes accessed | tf_op | source)
XLA Modules:
  0.0 60.2 jit_solution(12083556767495195640)
XLA Ops:
  1.9 56.5 %shard_map.92 = (f32[8,128]{1,0:T(8,128)}, f32[32,1152]{1,0:T(8,128)}, f32[32,1152]{1,0:T(8,128)}) custom-call(bf16[32,1152]{1,0:T(8,128)(2,1)} %img_hbm.1, bf16[32,1152]{1,0:T(8,128)(2,1)} %txt_hbm.1, s32[128]{0:T(128)} %counts_hbm.1, f32[1]{0:T(128)S(6)} %copy.10.log_temp_hbm, f32[1]{0:T(128)S(6)} %copy.11.bias_hbm), custom_call_target="tpu_custom_call" | custom-call | flops 3623878656 | bytes 4194304 | tf_op jit(solution)/shard_map/pallas_call | solution.py:479
  58.4 1.8 %shard_map.93 = (f32[1]{0:T(128)}, f32[1]{0:T(128)}, f32[1]{0:T(128)}, f32[32,1152]{1,0:T(8,128)}, f32[32,1152]{1,0:T(8,128)}) custom-call(f32[8,128]{1,0:T(8,128)} %get-tuple-element.8.scalars, f32[32,1152]{1,0:T(8,128)} %get-tuple-element.9.grad_img, f32[32,1152]{1,0:T(8,128)} %get-tuple-element.10.grad_txt), custom_call_target="tpu_custom_call" | custom-call | tf_op jit(solution)/shard_map/pallas_call | solution.py:512

commit v5 on v4

--- a/solution.py
+++ b/solution.py
@@ -12,8 +12,8 @@
 BF16 = jnp.bfloat16
 T = 32
 RING = 8
-N_SEM = 192
-SCAL = 160
+PIECES_OUT, CORE_OUT, PIECES_BACK, CORE_BACK, SCALARS_OUT, N_SENT = range(6)
+N_RECEIVED = 89
 FULL = (0, T)
 PIECES = ((0, 16), (16, 16))
 OWN, MATE = 0, 1
@@ -139,21 +139,32 @@
     txt_half = txt_unit.astype(BF16)
     txt[at(0), :] = txt_half
 
-    sent = []
-
-    def send(src, dst, peer):
-        index = len(sent)
-        made = pltpu.make_async_remote_copy(
+    rows_sent = [0] * N_SENT
+    used_sems = []
+
+    def fresh():
+        used_sems.append(len(used_sems))
+        return used_sems[-1]
+
+    def remote(src, dst, outgoing, index, peer):
+        return pltpu.make_async_remote_copy(
             src_ref=src,
             dst_ref=dst,
-            send_sem=ssem.at[index],
+            send_sem=ssem.at[outgoing],
             recv_sem=rsem.at[index],
             device_id=peer,
             device_id_type=MESH,
         )
-        made.start()
-        sent.append(made)
-        return made
+
+    def send(src, dst, peer, outgoing, index):
+        remote(src, dst, outgoing, index, peer).start()
+        rows_sent[outgoing] += src.shape[0]
+
+    def any_rows(rows):
+        return txt.at[pl.ds(0, rows)]
+
+    def wait_for(index, rows):
+        remote(any_rows(rows), any_rows(rows), 0, index, core_mate).wait_recv()
 
     odd = lax.rem(core, 2)
     TXT, IMG = 0, 1
@@ -168,7 +179,7 @@
 
     def move(ring, column, piece, k):
         buf, part = ring_buf[ring], PIECES[piece]
-        parent, made = ROUTES[piece][column][k], []
+        parent, index = ROUTES[piece][column][k], fresh()
         for way in ways(k):
             slot = ring_slot(k, way)
             if parent is None:
@@ -181,13 +192,13 @@
                 first = jnp.where(odd == 1, down, up) * T + part[0]
                 source, target = pl.ds(pl.multiple_of(first, 16), 16), at(column * 8 + slot, part)
                 peer = way_on(ring, k, parent)
-            made.append(send(buf.at[source], buf.at[target], peer))
-        gathered[ring, column, piece, k] = made
+            send(buf.at[source], buf.at[target], peer, PIECES_OUT, index)
+        gathered[ring, column, piece, k] = (index, part[1] * len(ways(k)))
 
     def arrive(*key):
-        for made in gathered.get(key, ()):
-            made.wait_recv()
-        gathered[key] = ()
+        if gathered[key] is not None:
+            wait_for(*gathered[key])
+            gathered[key] = None
 
     def run(column, piece, k, rings=(0, 1)):
         if column == CORE:
@@ -197,10 +208,11 @@
             if k or base:
                 for n in range(2):
                     arrive(TXT, piece, n, k)
-            gathered[TXT, CORE, piece, k] = [
-                send(txt.at[at(base + ring_slot(k, way))], txt.at[at(16 + base + ring_slot(k, way))], core_mate)
-                for way in ways(k)
-            ]
+            index = fresh()
+            for way in ways(k):
+                slot = base + ring_slot(k, way)
+                send(txt.at[at(slot)], txt.at[at(16 + slot)], core_mate, CORE_OUT, index)
+            gathered[TXT, CORE, piece, k] = (index, T * len(ways(k)))
             return
         parent = ROUTES[piece][column][k]
         for n in rings:
@@ -284,12 +296,27 @@
             scaled_sum = scaled_sum + used * folded(slope * scaled)
         return pair_sum, slope_sum, scaled_sum
 
+    def rows_of(group):
+        return pl.ds(group * 128, 128)
+
+    def text_dir(first):
+        return jnp.dot(weight[first : first + 128, :], img[...], preferred_element_type=F32)
+
+    core_back = {}
+
+    def other_texts(group):
+        out_c[rows_of(group), :] = text_dir(512 + group * 128).astype(BF16)
+        core_back[group] = fresh()
+        send(out_c.at[rows_of(group)], from_c.at[rows_of(group)], core_mate, CORE_BACK, core_back[group])
+
     zero = jnp.zeros((8, 512), F32)
     totals = (zero, zero, zero)
     for c in range(4):
         arrive_texts(c)
-    for c in (1, 0, 3, 2):
+    for c in (3, 2, 1, 0):
         totals = block(c, totals)
+        if c == 2:
+            other_texts(0)
     pair_sum, slope_sum, scaled_sum = totals
 
     lane = lax.broadcasted_iota(jnp.int32, (8, 128), 1)
@@ -304,44 +331,21 @@
             vector = jnp.where(lane == k, whole[k] + own_sums[k], vector)
         return vector
 
-    scal_sent = []
-
-    def scalar_copy(stage, d, mine, slot, peer):
-        return pltpu.make_async_remote_copy(
-            src_ref=scal.at[stage, mine],
-            dst_ref=scal.at[stage, slot],
-            send_sem=ssem.at[SCAL + stage * 8 + d],
-            recv_sem=rsem.at[SCAL + stage * 8 + slot],
-            device_id=peer,
-            device_id_type=MESH,
-        )
+    stage_sems = [fresh() for _ in range(3)]
 
     def spread(stage, mine, peer_of, value):
-        scal[stage, mine] = value
+        place = scal.at[stage * 8 + mine]
+        place[...] = value
         for d in range(1, RING):
-            made = scalar_copy(stage, d, mine, mine, peer_of(d))
-            made.start()
-            scal_sent.append(made)
-
-    def summed(stage, mine, peer_of):
-        for d in range(1, RING):
-            scalar_copy(stage, d, mine, ring(mine + d), peer_of(d)).wait_recv()
-        total = scal[stage, 0]
+            remote(place, place, SCALARS_OUT, stage_sems[stage], peer_of(d)).start()
+
+    def summed(stage):
+        others = scal.at[pl.ds(0, RING - 1)]
+        remote(others, others, SCALARS_OUT, stage_sems[stage], core_mate).wait_recv()
+        total = scal[stage * 8]
         for k in range(1, RING):
-            total = total + scal[stage, k]
+            total = total + scal[stage * 8 + k]
         return total
-
-    def rows_of(group):
-        return pl.ds(group * 128, 128)
-
-    def text_dir(first):
-        return jnp.dot(weight[first : first + 128, :], img[...], preferred_element_type=F32)
-
-    core_back = {}
-
-    def other_texts(group):
-        out_c[rows_of(group), :] = text_dir(512 + group * 128).astype(BF16)
-        core_back[group] = send(out_c.at[rows_of(group)], from_c.at[rows_of(group)], core_mate)
 
     def own_images(group):
         img_sum[rows_of(group), :] = lax.dot_general(
@@ -373,7 +377,7 @@
             return img_sum[at(slot, part), :]
         if group not in core_seen:
             core_seen.add(group)
-            core_back[group].wait_recv()
+            wait_for(core_back[group], 128)
         return txt_sum[at(slot, part), :] + from_c[at(slot, part), :].astype(F32)
 
     out, back = (txt_out, img_out), (txt_back, img_back)
@@ -384,9 +388,9 @@
         return pl.ds(row, 16)
 
     def received(ring, column, piece, k, way):
-        key = (ring, column, piece, k, way)
+        key = (ring, column, piece, k)
         if coming[key] is not None:
-            coming[key].wait_recv()
+            wait_for(*coming[key])
             coming[key] = None
         return back[ring][landing(column, piece, k, way), :].astype(F32)
 
@@ -406,7 +410,7 @@
         return value
 
     def pass_back(ring, column, piece, k):
-        parent, part = ROUTES[piece][column][k], PIECES[piece]
+        parent, part, index = ROUTES[piece][column][k], PIECES[piece], fresh()
         for way in ways(k):
             slot = column * 8 + ring_slot(k, way)
             out[ring][at(slot, part), :] = partial(ring, column, piece, k, way).astype(BF16)
@@ -417,10 +421,10 @@
             else:
                 peer = ring_peer[ring](jnp.where(odd == 1, k - parent, parent - k))
             target = back[ring].at[landing(column, piece, k, way)]
-            coming[ring, column, piece, k, way] = send(out[ring].at[at(slot, part)], target, peer)
+            send(out[ring].at[at(slot, part)], target, peer, PIECES_BACK, index)
+        coming[ring, column, piece, k] = (index, part[1] * len(ways(k)))
 
     ahead = 0
-    other_texts(0)
     for n in range(len(REDUCE) + ahead):
         if n < len(REDUCE):
             pass_back(IMG, *REDUCE[n])
@@ -429,11 +433,11 @@
         if n == 3:
             spread(0, y, y_peer, own_total())
         elif n == 10:
-            spread(1, z, z_peer, summed(0, y, y_peer))
+            spread(1, z, z_peer, summed(0))
         elif n == 15:
-            spread(2, my_xc, xc_peer, summed(1, z, z_peer))
-
-    total = summed(2, my_xc, xc_peer)
+            spread(2, my_xc, xc_peer, summed(1))
+
+    total = summed(2)
     means = total / used
     scalars[...] = means
 
@@ -444,9 +448,12 @@
         total_dir = jnp.concatenate([top, low], axis=0) + own_weight * other
         grad[...] = projected(total_dir, unit, length)
 
-    assert len(sent) <= SCAL and len(places) * 16 <= back[0].shape[0]
-    for made in sent + scal_sent:
-        made.wait_send()
+    assert len(used_sems) == N_RECEIVED and len(places) * 16 <= back[0].shape[0]
+    for kind, rows in enumerate(rows_sent):
+        if rows:
+            remote(any_rows(rows), any_rows(rows), kind, 0, core_mate).wait_send()
+    scalars_sent = scal.at[pl.ds(0, 3 * (RING - 1))]
+    remote(scalars_sent, scalars_sent, SCALARS_OUT, 0, core_mate).wait_send()
 
 
 def place_results(scalars, grad_img, grad_txt, loss, grad_log_temp, grad_bias, img_out, txt_out, staged, arrived):
@@ -499,10 +506,10 @@
             pltpu.VMEM((512, width), BF16),
             pltpu.VMEM((480, width), BF16),
             pltpu.VMEM((480, width), BF16),
-            pltpu.VMEM((3, 8, 8, 128), F32),
+            pltpu.VMEM((24, 8, 128), F32),
             pltpu.SemaphoreType.DMA((5,)),
-            pltpu.SemaphoreType.DMA((N_SEM,)),
-            pltpu.SemaphoreType.DMA((N_SEM,)),
+            pltpu.SemaphoreType.DMA((N_SENT,)),
+            pltpu.SemaphoreType.DMA((N_RECEIVED,)),
         ],
         compiler_params=pltpu.CompilerParams(
             collective_id=0, has_side_effects=True, vmem_limit_bytes=60 << 20

time: 60.6 us -> 57.1 us (0.942)
  Pallas kernels: 58.3 us -> 55 us
    pallas_call x1, Pallas kernels: 56.5 us -> 53.2 us  [body(): pl.pallas_call(kernel, out_shape=(jax.ShapeDtypeStruct((8, 128), F32), gr...]
where the time goes in v5:
time: 57.1 us; the launch traced here: 56.9 us
  Pallas kernels  55 us (96%)
  between operations  1.93 us (3%)
    pallas_call x1, Pallas kernels, body(): pl.pallas_call(kernel, out_shape=(jax.ShapeDtypeStruct((8, 128), F32), gr...  53.2 us
    pallas_call x1, Pallas kernels, body(): pl.pallas_call(place_results, out_shape=(scalar, scalar, scalar, grad, gr...  1.77 us

profile of v5, /device:TPU:1, one launch (start us, length us, event | category | flops | bytes accessed | tf_op | source)
XLA Modules:
  0.0 56.9 jit_solution(16390900165429169774)
XLA Ops:
  1.9 53.2 %shard_map.92 = (f32[8,128]{1,0:T(8,128)}, f32[32,1152]{1,0:T(8,128)}, f32[32,1152]{1,0:T(8,128)}) custom-call(bf16[32,1152]{1,0:T(8,128)(2,1)} %img_hbm.1, bf16[32,1152]{1,0:T(8,128)(2,1)} %txt_hbm.1, s32[128]{0:T(128)} %counts_hbm.1, f32[1]{0:T(128)S(6)} %copy.10.log_temp_hbm, f32[1]{0:T(128)S(6)} %copy.11.bias_hbm), custom_call_target="tpu_custom_call" | custom-call | flops 3623878656 | bytes 4194304 | tf_op jit(solution)/shard_map/pallas_call | solution.py:486
  55.2 1.8 %shard_map.93 = (f32[1]{0:T(128)}, f32[1]{0:T(128)}, f32[1]{0:T(128)}, f32[32,1152]{1,0:T(8,128)}, f32[32,1152]{1,0:T(8,128)}) custom-call(f32[8,128]{1,0:T(8,128)} %get-tuple-element.8.scalars, f32[32,1152]{1,0:T(8,128)} %get-tuple-element.9.grad_img, f32[32,1152]{1,0:T(8,128)} %get-tuple-element.10.grad_txt), custom_call_target="tpu_custom_call" | custom-call | tf_op jit(solution)/shard_map/pallas_call | solution.py:519

commit v6 on v5

--- a/solution.py
+++ b/solution.py
@@ -426,10 +426,10 @@
 
     ahead = 0
     for n in range(len(REDUCE) + ahead):
+        if n >= ahead:
+            pass_back(TXT, *REDUCE[n - ahead])
         if n < len(REDUCE):
             pass_back(IMG, *REDUCE[n])
-        if n >= ahead:
-            pass_back(TXT, *REDUCE[n - ahead])
         if n == 3:
             spread(0, y, y_peer, own_total())
         elif n == 10:

time: 57.1 us -> 57.2 us (level)
  no operation moved by 1% of the time
where the time goes in v6:
time: 57.2 us; the launch traced here: 57 us
  Pallas kernels  55.1 us (96%)
  between operations  1.93 us (3%)
    pallas_call x1, Pallas kernels, body(): pl.pallas_call(kernel, out_shape=(jax.ShapeDtypeStruct((8, 128), F32), gr...  53.4 us
    pallas_call x1, Pallas kernels, body(): pl.pallas_call(place_results, out_shape=(scalar, scalar, scalar, grad, gr...  1.77 us

profile of v6, /device:TPU:1, one launch (start us, length us, event | category | flops | bytes accessed | tf_op | source)
XLA Modules:
  0.0 57.0 jit_solution(8885068263242438718)
XLA Ops:
  1.9 53.4 %shard_map.92 = (f32[8,128]{1,0:T(8,128)}, f32[32,1152]{1,0:T(8,128)}, f32[32,1152]{1,0:T(8,128)}) custom-call(bf16[32,1152]{1,0:T(8,128)(2,1)} %img_hbm.1, bf16[32,1152]{1,0:T(8,128)(2,1)} %txt_hbm.1, s32[128]{0:T(128)} %counts_hbm.1, f32[1]{0:T(128)S(6)} %copy.10.log_temp_hbm, f32[1]{0:T(128)S(6)} %copy.11.bias_hbm), custom_call_target="tpu_custom_call" | custom-call | flops 3623878656 | bytes 4194304 | tf_op jit(solution)/shard_map/pallas_call | solution.py:486
  55.3 1.8 %shard_map.93 = (f32[1]{0:T(128)}, f32[1]{0:T(128)}, f32[1]{0:T(128)}, f32[32,1152]{1,0:T(8,128)}, f32[32,1152]{1,0:T(8,128)}) custom-call(f32[8,128]{1,0:T(8,128)} %get-tuple-element.8.scalars, f32[32,1152]{1,0:T(8,128)} %get-tuple-element.9.grad_img, f32[32,1152]{1,0:T(8,128)} %get-tuple-element.10.grad_txt), custom_call_target="tpu_custom_call" | custom-call | tf_op jit(solution)/shard_map/pallas_call | solution.py:519
